TPU v7x, 1024 devices: a whole 4x8x16 slice. The times are simulated.
1024 devices in a mesh: dp: 16 (over y_hi, x, core), expert: 64 (over z, y_lo).
Axes of the slice: x: 4, y: 8 (y_hi: 2, y_lo: 4; y = y_hi * 4 + y_lo), z: 16, core: 2. Of those that a mesh axis runs over, the one named last changes fastest.
Arguments:
- hidden_acts: bfloat16 [16, 64, 128, 512], P('dp', 'expert'), may hold values from -6 to 6
- token_gradients: bfloat16 [16, 64, 32, 2, 3584], P('dp', 'expert'), may hold values from -0.09375 to 0.09375
- local_hidden: bfloat16 [16, 64, 128, 512], P('dp', 'expert'), may hold values from -6 to 6
- local_grads: bfloat16 [16, 64, 128, 3584], P('dp', 'expert'), may hold values from -0.09375 to 0.09375
- counts: int32 [16, 64, 32], P('dp'), may hold values from 0 to 2, as said below
- weight: float32 [64, 512, 3584], P('expert', 'dp'), may hold values from -0.1875 to 0.1875
- moment: bfloat16 [64, 512, 3584], P('expert', 'dp'), may hold values from -2.5 to 2.5
- second: bfloat16 [64, 512, 3584], P('expert', 'dp'), may hold values from 0.049804688 to 2
Outputs:
- new_weight: float32 [64, 512, 3584], P('expert', 'dp')
- new_moment: bfloat16 [64, 512, 3584], P('expert', 'dp')
- new_second: bfloat16 [64, 512, 3584], P('expert', 'dp')
Inputs may be any that keep to these rules, and one draw needn't show every extreme that they name: `counts`: A source fills its slots for an expert from the first on. In every replica each expert has some source with all 2 slots filled, and one expert has all slots of every source filled.
All inputs are finite; a program needn't handle non-finite values.
Results may differ from a plain program's by a relative error of at most 0.009.
Values may be sent and summed in bfloat16 or wider, within the bound.
No kernel may reach another device: no remote copies, remote signals or barrier semaphores. Data moves between devices by JAX's collectives and lax.ppermute only.
A program may use at most 64 MiB of HBM per device.

v0:
```python
import jax
import jax.numpy as jnp
from jax import lax
from jax.sharding import PartitionSpec as P

PAIR = 2


beta_one = 0.9
beta_two = 0.95
learn_rate = 0.00022
decay_rate = 0.1
epsilon = 1e-08
correct_one = 1.0 - 0.9**20
correct_two = 1.0 - 0.95**20


def contract_rows(left_rows, right_rows):
    return lax.dot_general(
        left_rows, right_rows, (((0,), (0,)), ((), ())), preferred_element_type=jnp.float32
    )


def on_device(
    hidden_acts, token_gradients, local_hidden, local_grads, counts, weight, moment, second
):
    device_index = lax.axis_index("expert")
    expert_id = device_index // PAIR
    outgoing = token_gradients[0, 0]
    experts, slot_count, feature_count = outgoing.shape
    copies = jnp.repeat(outgoing, PAIR, axis=0)
    arrived = lax.all_to_all(copies, "expert", split_axis=0, concat_axis=0, tiled=True)
    sources = arrived.shape[0]
    capacity = sources * slot_count
    gradient_row_block = arrived.reshape(capacity, feature_count)
    filled = lax.dynamic_index_in_dim(counts[0], expert_id, axis=1, keepdims=False)
    slot_ids = jnp.arange(slot_count, dtype=jnp.int32)
    is_live = (slot_ids[None, :] < filled[:, None]).reshape(capacity)
    hidden_state = hidden_acts[0, 0]
    owned_hidden_state = local_hidden[0, 0]
    owned_gradients = local_grads[0, 0]
    kept_hidden = jnp.where(is_live[:, None], hidden_state, jnp.zeros_like(hidden_state))
    summed = lax.psum_scatter(
        (
            contract_rows(kept_hidden, gradient_row_block)
            + contract_rows(owned_hidden_state, owned_gradients)
        ).astype(jnp.bfloat16),
        "dp",
        scatter_dimension=0,
        tiled=True,
    ).astype(jnp.float32)
    moment_new = beta_one * moment[0].astype(jnp.float32) + (1.0 - beta_one) * summed
    second_new = beta_two * second[0].astype(jnp.float32) + (1.0 - beta_two) * summed * summed
    step_direction = moment_new / correct_one / (jnp.sqrt(second_new / correct_two) + epsilon)
    master = weight[0]
    new_weight = master - learn_rate * (step_direction + decay_rate * master)
    return (
        new_weight[None],
        moment_new.astype(jnp.bfloat16)[None],
        second_new.astype(jnp.bfloat16)[None],
    )


def solution(mesh):
    placed = (
        P("dp", "expert", None, None),
        P("dp", "expert", None, None, None),
        P("dp", "expert", None, None),
        P("dp", "expert", None, None),
        P("dp", None, None),
        P("expert", "dp", None),
        P("expert", "dp", None),
        P("expert", "dp", None),
    )
    return jax.shard_map(
        on_device,
        mesh=mesh,
        in_specs=placed,
        out_specs=(P("expert", "dp", None), P("expert", "dp", None), P("expert", "dp", None)),
        check_vma=False,
    )
```

profile of v0, /device:TPU:8, one launch (start us, length us, event | category | flops | bytes accessed | tf_op | source)
XLA Modules:
  0.0 210.4 jit_solution(5879728444165417204)
XLA Ops:
  7.2 0.0 copy-start
  7.2 0.0 copy-start.4
  7.2 2.5 %broadcast_in_dim.27 = bf16[32,2,2,3584]{3,2,1,0:T(2,128)(2,1)} broadcast(bf16[32,2,3584]{2,1,0:T(2,128)(2,1)} %bitcast.47), dimensions={0,2,3} | broadcast | bytes 1376256 | tf_op jit(solution)/shard_map/broadcast_in_dim | solution.py:31
  9.7 22.8 %all-to-all-start = ((bf16[64,2,3584]{2,1,0:T(2,128)(2,1)}), bf16[64,2,3584]{2,1,0:T(2,128)(2,1)S(1)}, u32[]{:S(2)}, u32[]{:S(2)}) async-start(bf16[64,2,3584]{2,1,0:T(2,128)(2,1)} %bitcast.5), calls=%async_computation | async-start | bytes 1835008 | tf_op jit(solution)/shard_map/all_to_all | solution.py:32
  32.5 0.0 reduce-scatter.2.cloned.1.call-start
  32.6 0.7 dynamic-slice_bitcast_fusion
  33.3 0.1 iota_compare_fusion
  33.4 0.2 lt.31
  33.5 48.6 %all-to-all-done = bf16[64,2,3584]{2,1,0:T(2,128)(2,1)S(1)} async-done(((bf16[64,2,3584]{2,1,0:T(2,128)(2,1)}), bf16[64,2,3584]{2,1,0:T(2,128)(2,1)S(1)}, u32[]{:S(2)}, u32[]{:S(2)}) %all-to-all-start) | async-done | bytes 917536 | tf_op jit(solution)/shard_map/all_to_all | solution.py:32
  82.1 0.3 reshape.43
  82.4 2.1 %fusion.11 = f32[512,3584]{1,0:T(8,128)S(1)} fusion(bf16[128,3584]{1,0:T(8,128)(2,1)S(1)} %reshape.43, bf16[1,1,128,512]{3,2,1,0:T(8,128)(2,1)} %param.8, pred[128]{0:T(512)(128)(4,1)S(1)} %lt.31), kind=kOutput, calls=%fused_computation.16 | convolution fusion | flops 469827584 | bytes 8388736 | tf_op jit(solution)/shard_map/dot_general | solution.py:19
  84.5 0.0 copy-done
  84.6 0.0 copy-done.4
  84.6 0.0 copy-start.1
  84.6 0.0 copy-start.2
  84.6 0.0 copy-start.3
  84.6 3.0 %add_convert_fusion = bf16[512,3584]{1,0:T(8,128)(2,1)} fusion(f32[512,3584]{1,0:T(8,128)S(1)} %fusion.11, bf16[1,1,128,3584]{3,2,1,0:T(8,128)(2,1)S(1)} %copy-done, bf16[1,1,128,512]{3,2,1,0:T(8,128)(2,1)S(1)} %copy-done.4), kind=kOutput, calls=%fused_computation | convolution fusion | flops 473432064 | bytes 12058624 | tf_op jit(solution)/shard_map/dot_general | solution.py:19
  87.5 0.0 reduce-scatter.2.cloned.1.call-update
  87.6 113.6 %reduce-scatter.2.cloned.1.call-done = bf16[32,3584]{1,0:T(8,128)(2,1)} async-done(((bf16[512,3584]{1,0:T(8,128)(2,1)}), bf16[32,3584]{1,0:T(8,128)(2,1)}) %reduce-scatter.2.cloned.1.call-update) | async-done | bytes 229392 | tf_op jit(solution)/shard_map/reduce_scatter | solution.py:43
  201.1 0.0 copy-done.1
  201.1 0.0 copy-done.2
  201.1 0.0 copy-done.3
  201.1 2.4 %fusion.8 = (bf16[1,32,3584]{2,1,0:T(8,128)(2,1)}, f32[1,32,3584]{2,1,0:T(8,128)}, bf16[1,32,3584]{2,1,0:T(8,128)(2,1)}) fusion(bf16[32,3584]{1,0:T(8,128)(2,1)} %reduce-scatter.2.cloned.1.call-done, bf16[1,32,3584]{2,1,0:T(8,128)(2,1)S(1)} %copy-done.2, bf16[1,32,3584]{2,1,0:T(8,128)(2,1)S(1)} %copy-done.3, f32[1,32,3584]{2,1,0:T(8,128)S(1)} %copy-done.1), kind=kLoop, calls=%fused_computation.13 | loop fusion | flops 2293760 | bytes 2064384 | tf_op jit(solution)/shard_map/broadcast_in_dim | solution.py:60
Async XLA Ops:
  7.2 77.4 %copy-start = (bf16[1,1,128,3584]{3,2,1,0:T(8,128)(2,1)S(1)}, bf16[1,1,128,3584]{3,2,1,0:T(8,128)(2,1)}, u32[]{:S(2)}) copy-start(bf16[1,1,128,3584]{3,2,1,0:T(8,128)(2,1)} %param.11) | copy-start | bytes 2752516
  7.2 77.4 %copy-start.4 = (bf16[1,1,128,512]{3,2,1,0:T(8,128)(2,1)S(1)}, bf16[1,1,128,512]{3,2,1,0:T(8,128)(2,1)}, u32[]{:S(2)}) copy-start(bf16[1,1,128,512]{3,2,1,0:T(8,128)(2,1)} %param.10) | copy-start | bytes 393220
  9.7 72.4 %all-to-all-start = ((bf16[64,2,3584]{2,1,0:T(2,128)(2,1)}), bf16[64,2,3584]{2,1,0:T(2,128)(2,1)S(1)}, u32[]{:S(2)}, u32[]{:S(2)}) async-start(bf16[64,2,3584]{2,1,0:T(2,128)(2,1)} %bitcast.5), calls=%async_computation | async-start | bytes 1835008 | tf_op jit(solution)/shard_map/all_to_all | solution.py:32
  32.5 168.6 %reduce-scatter.2.cloned.1.call-start = ((), (), s32[]{:S(2)}) async-start(), calls=%async_computation.2 | async-start | bytes 3899392 | tf_op jit(solution)/shard_map/reduce_scatter | solution.py:43
  84.6 116.6 %copy-start.1 = (f32[1,32,3584]{2,1,0:T(8,128)S(1)}, f32[1,32,3584]{2,1,0:T(8,128)}, u32[]{:S(2)}) copy-start(f32[1,32,3584]{2,1,0:T(8,128)} %param.13) | copy-start | bytes 1376260
  84.6 116.6 %copy-start.2 = (bf16[1,32,3584]{2,1,0:T(8,128)(2,1)S(1)}, bf16[1,32,3584]{2,1,0:T(8,128)(2,1)}, u32[]{:S(2)}) copy-start(bf16[1,32,3584]{2,1,0:T(8,128)(2,1)} %param.15) | copy-start | bytes 688132
  84.6 116.6 %copy-start.3 = (bf16[1,32,3584]{2,1,0:T(8,128)(2,1)S(1)}, bf16[1,32,3584]{2,1,0:T(8,128)(2,1)}, u32[]{:S(2)}) copy-start(bf16[1,32,3584]{2,1,0:T(8,128)(2,1)} %param.14) | copy-start | bytes 688132
Sparse Core Ops, SparseCore 0:
  87.7 113.4 reduce-scatter.1
where the time goes:
time: 211 us; the launch traced here: 210 us
  waiting for transfers between devices  162 us (77%)
  starting transfers between devices  22.8 us (11%)
  between operations  14.1 us (7%)
  matrix products  5.06 us (2%)
  local copies, waits for them, and re-layouts  3.74 us (2%)
  other arithmetic  2.44 us (1%)
    reduce_scatter x1, waiting for transfers between devices, on_device(): lax.psum_scatter((contract_rows(kept_hidden, gradient_row_block) + contra...  114 us
    all_to_all x1, waiting for transfers between devices, on_device(): lax.all_to_all(copies, 'expert', split_axis=0, concat_axis=0, tiled=True)  48.6 us
    all_to_all x1, starting transfers between devices, on_device(): lax.all_to_all(copies, 'expert', split_axis=0, concat_axis=0, tiled=True)  22.8 us
    dot_general x2, matrix products, contract_rows(): lax.dot_general(left_rows, right_rows, (((0,), (0,)), ((), ())), preferre...  5.06 us
  transfers between devices with their start and end apart: 2, of which 2 were waited for; matrix products, arithmetic and copies ran while one was open for 0% of the time, Pallas kernels for 0%

commit v1 on v0

v1 whole, which is shorter than its diff:
```python
import jax
import jax.numpy as jnp
from jax import lax
from jax.sharding import Mesh, PartitionSpec as P

AXES = ("y_hi", "x", "core", "z", "y_half", "y_low")

beta_one = 0.9
beta_two = 0.95
learn_rate = 0.00022
decay_rate = 0.1
epsilon = 1e-08
correct_one = 1.0 - 0.9**20
correct_two = 1.0 - 0.95**20


def contract_rows(left_rows, right_rows):
    return lax.dot_general(
        left_rows, right_rows, (((0,), (0,)), ((), ())), preferred_element_type=jnp.float32
    )


def swap(block, axis, pairs):
    return lax.ppermute(block, axis, pairs + [(b, a) for a, b in pairs])


def flip_if(condition, block, axis):
    return jnp.where(condition, jnp.flip(block, axis), block)


def on_device(
    hidden_acts, token_gradients, local_hidden, local_grads, counts, weight, moment, second
):
    core = lax.axis_index("core")
    low = lax.axis_index("y_low")
    expert_id = lax.axis_index("z") * 2 + lax.axis_index("y_half")
    features = token_gradients.shape[-1]
    n_chunks = 2
    per_core = features // 2
    width = per_core // n_chunks
    n_z = 16
    slots = token_gradients.shape[3]
    units = hidden_acts.shape[-1]

    outgoing = token_gradients[0, 0].reshape(n_z, 2, slots, 2, n_chunks, width)
    arrived = [
        lax.all_to_all(
            outgoing[:, :, :, :, chunk].transpose(3, 0, 1, 2, 4).reshape(-1, slots, width),
            ("core", "z", "y_half"),
            0,
            0,
            tiled=True,
        )
        for chunk in range(n_chunks)
    ]

    filled = lax.dynamic_index_in_dim(counts[0], expert_id, axis=1, keepdims=False)
    slot_ids = jnp.arange(slots, dtype=jnp.int32)
    is_live = (slot_ids[None, :] < filled[:, None]).reshape(-1)
    hidden = hidden_acts[0, 0]
    hidden = jnp.where(is_live[:, None], hidden, jnp.zeros_like(hidden))
    hidden = hidden.reshape(n_z, 2, 2, slots, units)
    hidden = flip_if(low == 1, hidden, 2)
    hidden = hidden.reshape(-1, units)
    both = jnp.concatenate([hidden, local_hidden[0, 0]], axis=0)
    both = both.reshape(-1, 2, 4, units // 8).transpose(0, 2, 1, 3).reshape(-1, units)
    both_other = swap(both, "core", [(0, 1)])
    rows = hidden.shape[0]
    first = jnp.where(core == 0, both[:rows], both_other[:rows])
    last = jnp.where(core == 0, both_other[:rows], both[:rows])
    routed = jnp.stack([first, last]).reshape(2, n_z, 2, 2, slots, units)
    routed = routed.transpose(3, 0, 1, 2, 4, 5).reshape(2 * rows, units)
    owned = jnp.concatenate([both[rows:], both_other[rows:]], axis=0)

    grads = local_grads[0, 0].reshape(-1, 2, per_core)
    grads_other = swap(
        lax.dynamic_index_in_dim(grads, 1 - core, 1, keepdims=False), "core", [(0, 1)]
    )
    grads_mine = lax.dynamic_index_in_dim(grads, core, 1, keepdims=False)
    grads_both = jnp.concatenate([grads_mine, grads_other], axis=0)

    def reduce_chunk(left, right, chunk):
        local = grads_both[:, chunk * width : (chunk + 1) * width]
        partial = contract_rows(left, right) + contract_rows(owned, local)
        partial = partial.astype(jnp.bfloat16).reshape(4, units // 4, width)
        partial = lax.all_to_all(partial, "x", 0, 0, tiled=True)
        summed = jnp.sum(partial.astype(jnp.float32), axis=0).astype(jnp.bfloat16)
        summed = summed.reshape(4, units // 16, width)
        summed = lax.all_to_all(summed, ("y_hi", "core"), 0, 0, tiled=True)
        summed = summed.astype(jnp.float32)
        return summed[:2] + summed[2:]

    grads_summed = []
    for chunk in range(n_chunks):
        near = arrived[chunk].reshape(-1, width)
        far = swap(near, "y_low", [(0, 1)])
        grads_summed.append(
            reduce_chunk(routed, jnp.concatenate([near, far], axis=0), chunk)
        )
    summed = jnp.concatenate(
        [grads_summed[chunk][side] for side in range(2) for chunk in range(n_chunks)], axis=-1
    )
    moment_new = beta_one * moment[0].astype(jnp.float32) + (1.0 - beta_one) * summed
    second_new = beta_two * second[0].astype(jnp.float32) + (1.0 - beta_two) * summed * summed
    step_direction = moment_new / correct_one / (jnp.sqrt(second_new / correct_two) + epsilon)
    master = weight[0]
    new_weight = master - learn_rate * (step_direction + decay_rate * master)
    return (
        new_weight[None],
        moment_new.astype(jnp.bfloat16)[None],
        second_new.astype(jnp.bfloat16)[None],
    )


def solution(mesh):
    dp = ("y_hi", "x", "core")
    expert = ("z", "y_half", "y_low")
    fine = Mesh(mesh.devices.reshape(2, 4, 2, 16, 2, 2), AXES)
    outs = P(expert, dp, None)
    return jax.shard_map(
        on_device,
        mesh=fine,
        in_specs=(
            P(dp, expert, None, None),
            P(dp, expert, None, None, None),
            P(dp, expert, None, None),
            P(dp, expert, None, None),
            P(dp, None, None),
            outs,
            outs,
            outs,
        ),
        out_specs=(outs, outs, outs),
        check_vma=False,
    )
```

time: 211 us -> 140 us (0.66)
  the two profiles are of different devices: /device:TPU:8 before, /device:TPU:9 now
where the time goes in v1:
time: 140 us
  waiting for transfers between devices  67.5 us (48%)
  starting transfers between devices  54.4 us (39%)
  local copies, waits for them, and re-layouts  7.45 us (5%)
  other arithmetic  5.51 us (4%)
  matrix products  3.73 us (3%)
    all_to_all x2, starting transfers between devices, on_device(): lax.all_to_all(outgoing[:, :, :, :, chunk].transpose(3, 0, 1, 2, 4).resha...  28.1 us
    all_to_all x2, waiting for transfers between devices, reduce_chunk(): summed = lax.all_to_all(summed, ('y_hi', 'core'), 0, 0, tiled=True)  21.1 us
    all_to_all x2, waiting for transfers between devices, on_device(): lax.all_to_all(outgoing[:, :, :, :, chunk].transpose(3, 0, 1, 2, 4).resha...  17.7 us
    all_to_all x2, waiting for transfers between devices, reduce_chunk(): partial = lax.all_to_all(partial, 'x', 0, 0, tiled=True)  15.3 us
    ppermute x4, waiting for transfers between devices, swap(): return lax.ppermute(block, axis, pairs + [(b, a) for a, b in pairs])  13.4 us
    all_to_all x2, starting transfers between devices, reduce_chunk(): summed = lax.all_to_all(summed, ('y_hi', 'core'), 0, 0, tiled=True)  10.3 us
    ppermute x4, starting transfers between devices, swap(): return lax.ppermute(block, axis, pairs + [(b, a) for a, b in pairs])  8.48 us
    all_to_all x2, starting transfers between devices, reduce_chunk(): partial = lax.all_to_all(partial, 'x', 0, 0, tiled=True)  7.52 us
  transfers between devices with their start and end apart: 10, of which 8 were waited for; matrix products, arithmetic and copies ran while one was open for 9% of the time, Pallas kernels for 0%

profile of v1, /device:TPU:9, one launch (start us, length us, event | category | flops | bytes accessed | tf_op | source)
XLA Modules:
  0.0 139.7 jit_solution(152908332470841351)
XLA Ops:
  0.6 1.3 reshape.227
  3.7 22.1 %all-to-all-start = ((bf16[64,2,896]{2,1,0:T(2,128)(2,1)}), bf16[64,2,896]{2,1,0:T(2,128)(2,1)S(1)}, u32[]{:S(2)}, u32[]{:S(2)}) async-start(bf16[64,2,896]{2,1,0:T(2,128)(2,1)} %bitcast.7), calls=%async_computation | async-start | bytes 458752 | tf_op jit(solution)/shard_map/all_to_all | solution.py:47
  27.8 2.3 %collective-permute-start = (bf16[256,512]{0,1:T(8,128)(2,1)S(1)}, bf16[256,512]{0,1:T(8,128)(2,1)}, u32[]{:S(2)}, u32[]{:S(2)}) collective-permute-start(bf16[256,512]{0,1:T(8,128)(2,1)S(1)} %bitcast.38), channel_id=1, source_target_pairs={{0,64},{64,0},{1,65},{65,1},{2,66},{66,2},{3,67},{67,3},{4,68},{68... | collective-permute-start | bytes 786440 | tf_op jit(solution)/shard_map/ppermute | solution.py:24
  31.0 2.1 %collective-permute-start.2 = (bf16[128,1792]{1,0:T(8,128)(2,1)S(1)}, bf16[128,1792]{1,0:T(8,128)(2,1)S(1)}, u32[]{:S(2)}, u32[]{:S(2)}) collective-permute-start(bf16[128,1792]{1,0:T(8,128)(2,1)S(1)} %bitcast.37), channel_id=1, source_target_pairs={{0,64},{64,0},{1,65},{65,1},{2,66},{66,2},{3,67},{67,3},{4,68},{68... | collective-permute-start | bytes 1376264 | tf_op jit(solution)/shard_map/ppermute | solution.py:24
  33.9 11.7 %all-to-all-done = bf16[64,2,896]{2,1,0:T(2,128)(2,1)S(1)} async-done(((bf16[64,2,896]{2,1,0:T(2,128)(2,1)}), bf16[64,2,896]{2,1,0:T(2,128)(2,1)S(1)}, u32[]{:S(2)}, u32[]{:S(2)}) %all-to-all-start) | async-done | bytes 229408 | tf_op jit(solution)/shard_map/all_to_all | solution.py:47
  45.6 6.0 %all-to-all-start.3 = ((bf16[64,2,896]{2,1,0:T(2,128)(2,1)}), bf16[64,2,896]{2,1,0:T(2,128)(2,1)S(1)}, u32[]{:S(2)}, u32[]{:S(2)}) async-start(bf16[64,2,896]{2,1,0:T(2,128)(2,1)} %bitcast.16), calls=%async_computation.3 | async-start | bytes 458752 | tf_op jit(solution)/shard_map/all_to_all | solution.py:47
  52.4 1.0 bitcast_select_fusion.1
  53.9 2.1 %collective-permute-start.1 = (bf16[128,896]{1,0:T(8,128)(2,1)S(1)}, bf16[128,896]{1,0:T(8,128)(2,1)S(1)}, u32[]{:S(2)}, u32[]{:S(2)}) collective-permute-start(bf16[128,896]{1,0:T(8,128)(2,1)S(1)} %reshape.220), channel_id=1, source_target_pairs={{0,1},{1,0},{2,3},{3,2},{4,5},{5,4},{6,7},{7,6},{8,9},{9,8},{10,11... | collective-permute-start | bytes 688136 | tf_op jit(solution)/shard_map/ppermute | solution.py:24
  57.1 6.8 %collective-permute-done.1 = bf16[128,896]{1,0:T(8,128)(2,1)S(1)} collective-permute-done((bf16[128,896]{1,0:T(8,128)(2,1)S(1)}, bf16[128,896]{1,0:T(8,128)(2,1)S(1)}, u32[]{:S(2)}, u32[]{:S(2)}) %collective-permute-start.1) | collective-permute-done | bytes 229408 | tf_op jit(solution)/shard_map/ppermute | solution.py:24
  63.9 1.4 %add_convert_fusion.1 = bf16[512,896]{1,0:T(8,128)(2,1)} fusion(f32[512,896]{1,0:T(8,128)S(1)} %fusion.2, bf16[256,512]{1,0:T(8,128)(2,1)S(1)} %reshape.218, bf16[128,896]{1,0:T(8,128)(2,1)S(1)} %collective-permute-done.1, bf16[128,896]{1,0:T(8,128)(2,1)S(1)} %reshape.220), kind=kOutput, calls=%fused_computation.1 | convolution fusion | flops 236716032 | bytes 3473408 | tf_op jit(solution)/shard_map/dot_general | solution.py:18
  65.4 6.1 %all-to-all-done.3 = bf16[64,2,896]{2,1,0:T(2,128)(2,1)S(1)} async-done(((bf16[64,2,896]{2,1,0:T(2,128)(2,1)}), bf16[64,2,896]{2,1,0:T(2,128)(2,1)S(1)}, u32[]{:S(2)}, u32[]{:S(2)}) %all-to-all-start.3) | async-done | bytes 229408 | tf_op jit(solution)/shard_map/all_to_all | solution.py:47
  71.4 4.0 %all-to-all-start.1 = ((bf16[4,128,896]{2,1,0:T(8,128)(2,1)}), bf16[4,128,896]{2,1,0:T(8,128)(2,1)S(1)}, u32[]{:S(2)}, u32[]{:S(2)}) async-start(bf16[4,128,896]{2,1,0:T(8,128)(2,1)} %bitcast.12), calls=%async_computation.1 | async-start | bytes 1835008 | tf_op jit(solution)/shard_map/all_to_all | solution.py:86
  75.5 2.1 %collective-permute-start.3 = (bf16[128,896]{1,0:T(8,128)(2,1)S(1)}, bf16[128,896]{1,0:T(8,128)(2,1)S(1)}, u32[]{:S(2)}, u32[]{:S(2)}) collective-permute-start(bf16[128,896]{1,0:T(8,128)(2,1)S(1)} %reshape.224), channel_id=1, source_target_pairs={{0,1},{1,0},{2,3},{3,2},{4,5},{5,4},{6,7},{7,6},{8,9},{9,8},{10,11... | collective-permute-start | bytes 688136 | tf_op jit(solution)/shard_map/ppermute | solution.py:24
  78.1 6.6 %collective-permute-done.3 = bf16[128,896]{1,0:T(8,128)(2,1)S(1)} collective-permute-done((bf16[128,896]{1,0:T(8,128)(2,1)S(1)}, bf16[128,896]{1,0:T(8,128)(2,1)S(1)}, u32[]{:S(2)}, u32[]{:S(2)}) %collective-permute-start.3) | collective-permute-done | bytes 229408 | tf_op jit(solution)/shard_map/ppermute | solution.py:24
  84.6 1.4 %add_convert_fusion = bf16[512,896]{1,0:T(8,128)(2,1)} fusion(f32[512,896]{1,0:T(8,128)S(1)} %fusion.4, bf16[256,512]{1,0:T(8,128)(2,1)S(1)} %reshape.218, bf16[128,896]{1,0:T(8,128)(2,1)S(1)} %collective-permute-done.3, bf16[128,896]{1,0:T(8,128)(2,1)S(1)} %reshape.224), kind=kOutput, calls=%fused_computation | convolution fusion | flops 236716032 | bytes 3473408 | tf_op jit(solution)/shard_map/dot_general | solution.py:18
  86.0 3.2 %all-to-all-done.1 = bf16[4,128,896]{2,1,0:T(8,128)(2,1)S(1)} async-done(((bf16[4,128,896]{2,1,0:T(8,128)(2,1)}), bf16[4,128,896]{2,1,0:T(8,128)(2,1)S(1)}, u32[]{:S(2)}, u32[]{:S(2)}) %all-to-all-start.1) | async-done | bytes 917536 | tf_op jit(solution)/shard_map/all_to_all | solution.py:86
  89.3 3.5 %all-to-all-start.4 = ((bf16[4,128,896]{2,1,0:T(8,128)(2,1)}), bf16[4,128,896]{2,1,0:T(8,128)(2,1)S(1)}, u32[]{:S(2)}, u32[]{:S(2)}) async-start(bf16[4,128,896]{2,1,0:T(8,128)(2,1)} %bitcast.17), calls=%async_computation.4 | async-start | bytes 1835008 | tf_op jit(solution)/shard_map/all_to_all | solution.py:86
  92.8 0.9 reduce_sum.24
  93.6 12.0 %all-to-all-done.4 = bf16[4,128,896]{2,1,0:T(8,128)(2,1)S(1)} async-done(((bf16[4,128,896]{2,1,0:T(8,128)(2,1)}), bf16[4,128,896]{2,1,0:T(8,128)(2,1)S(1)}, u32[]{:S(2)}, u32[]{:S(2)}) %all-to-all-start.4) | async-done | bytes 917536 | tf_op jit(solution)/shard_map/all_to_all | solution.py:86
  105.7 6.1 %all-to-all-start.2 = ((bf16[4,32,896]{2,1,0:T(8,128)(2,1)}), bf16[4,32,896]{2,1,0:T(8,128)(2,1)S(1)}, u32[]{:S(2)}, u32[]{:S(2)}) async-start(bf16[4,32,896]{2,1,0:T(8,128)(2,1)} %bitcast.13), calls=%async_computation.2 | async-start | bytes 458752 | tf_op jit(solution)/shard_map/all_to_all | solution.py:89
  112.6 10.3 %all-to-all-done.2 = bf16[4,32,896]{2,1,0:T(8,128)(2,1)S(1)} async-done(((bf16[4,32,896]{2,1,0:T(8,128)(2,1)}), bf16[4,32,896]{2,1,0:T(8,128)(2,1)S(1)}, u32[]{:S(2)}, u32[]{:S(2)}) %all-to-all-start.2) | async-done | bytes 229408 | tf_op jit(solution)/shard_map/all_to_all | solution.py:89
  123.0 4.2 %all-to-all-start.5 = ((bf16[4,32,896]{2,1,0:T(8,128)(2,1)}), bf16[4,32,896]{2,1,0:T(8,128)(2,1)S(1)}, u32[]{:S(2)}, u32[]{:S(2)}) async-start(bf16[4,32,896]{2,1,0:T(8,128)(2,1)} %bitcast.18), calls=%async_computation.5 | async-start | bytes 458752 | tf_op jit(solution)/shard_map/all_to_all | solution.py:89
  127.3 10.8 %all-to-all-done.5 = bf16[4,32,896]{2,1,0:T(8,128)(2,1)S(1)} async-done(((bf16[4,32,896]{2,1,0:T(8,128)(2,1)}), bf16[4,32,896]{2,1,0:T(8,128)(2,1)S(1)}, u32[]{:S(2)}, u32[]{:S(2)}) %all-to-all-start.5) | async-done | bytes 229408 | tf_op jit(solution)/shard_map/all_to_all | solution.py:89
  138.2 1.4 %fusion.13 = (bf16[1,32,3584]{2,1,0:T(8,128)(2,1)}, f32[1,32,3584]{2,1,0:T(8,128)}, bf16[1,32,3584]{2,1,0:T(8,128)(2,1)}) fusion(f32[1,32,896]{2,1,0:T(8,128)S(1)} %get-tuple-element.18, f32[1,32,896]{2,1,0:T(8,128)S(1)} %get-tuple-element.16, f32[1,32,896]{2,1,0:T(8,128)S(1)} %get-tuple-element.17, f32[1,32,896]{2,1,0:T(8,128)S(1)} %get-tuple-element.15, ...), kind=kLoop, calls=%fused_computation.32 | loop fusion | flops 2523136 | bytes 2293760 | tf_op jit(solution)/shard_map/convert_element_type | solution.py:111
  (56 shorter events, 9.2 us)
Async XLA Ops:
  0.6 25.2 %copy-start = (s32[1,64,32]{1,2,0:T(8,128)S(1)}, s32[1,64,32]{1,2,0:T(8,128)}, u32[]{:S(2)}) copy-start(s32[1,64,32]{1,2,0:T(8,128)} %param.12) | copy-start | bytes 24580
  2.0 24.1 %copy-start.5 = (bf16[1,1,128,512]{3,2,1,0:T(8,128)(2,1)S(1)}, bf16[1,1,128,512]{3,2,1,0:T(8,128)(2,1)}, u32[]{:S(2)}) copy-start(bf16[1,1,128,512]{3,2,1,0:T(8,128)(2,1)} %param.8) | copy-start | bytes 393220
  2.6 24.1 %copy-start.6 = (bf16[1,1,128,512]{3,2,1,0:T(8,128)(2,1)S(1)}, bf16[1,1,128,512]{3,2,1,0:T(8,128)(2,1)}, u32[]{:S(2)}) copy-start(bf16[1,1,128,512]{3,2,1,0:T(8,128)(2,1)} %param.10) | copy-start | bytes 393220
  3.7 42.0 %all-to-all-start = ((bf16[64,2,896]{2,1,0:T(2,128)(2,1)}), bf16[64,2,896]{2,1,0:T(2,128)(2,1)S(1)}, u32[]{:S(2)}, u32[]{:S(2)}) async-start(bf16[64,2,896]{2,1,0:T(2,128)(2,1)} %bitcast.7), calls=%async_computation | async-start | bytes 458752 | tf_op jit(solution)/shard_map/all_to_all | solution.py:47
  26.1 4.0 %copy-start.1 = (bf16[1,1,128,3584]{3,2,1,0:T(8,128)(2,1)S(1)}, bf16[1,1,128,3584]{3,2,1,0:T(8,128)(2,1)}, u32[]{:S(2)}) copy-start(bf16[1,1,128,3584]{3,2,1,0:T(8,128)(2,1)} %param.11) | copy-start | bytes 2752516
  27.8 24.6 %collective-permute-start = (bf16[256,512]{0,1:T(8,128)(2,1)S(1)}, bf16[256,512]{0,1:T(8,128)(2,1)}, u32[]{:S(2)}, u32[]{:S(2)}) collective-permute-start(bf16[256,512]{0,1:T(8,128)(2,1)S(1)} %bitcast.38), channel_id=1, source_target_pairs={{0,64},{64,0},{1,65},{65,1},{2,66},{66,2},{3,67},{67,3},{4,68},{68... | collective-permute-start | bytes 786440 | tf_op jit(solution)/shard_map/ppermute | solution.py:24
  31.0 25.7 %collective-permute-start.2 = (bf16[128,1792]{1,0:T(8,128)(2,1)S(1)}, bf16[128,1792]{1,0:T(8,128)(2,1)S(1)}, u32[]{:S(2)}, u32[]{:S(2)}) collective-permute-start(bf16[128,1792]{1,0:T(8,128)(2,1)S(1)} %bitcast.37), channel_id=1, source_target_pairs={{0,64},{64,0},{1,65},{65,1},{2,66},{66,2},{3,67},{67,3},{4,68},{68... | collective-permute-start | bytes 1376264 | tf_op jit(solution)/shard_map/ppermute | solution.py:24
  45.6 25.8 %all-to-all-start.3 = ((bf16[64,2,896]{2,1,0:T(2,128)(2,1)}), bf16[64,2,896]{2,1,0:T(2,128)(2,1)S(1)}, u32[]{:S(2)}, u32[]{:S(2)}) async-start(bf16[64,2,896]{2,1,0:T(2,128)(2,1)} %bitcast.16), calls=%async_computation.3 | async-start | bytes 458752 | tf_op jit(solution)/shard_map/all_to_all | solution.py:47
  53.9 10.0 %collective-permute-start.1 = (bf16[128,896]{1,0:T(8,128)(2,1)S(1)}, bf16[128,896]{1,0:T(8,128)(2,1)S(1)}, u32[]{:S(2)}, u32[]{:S(2)}) collective-permute-start(bf16[128,896]{1,0:T(8,128)(2,1)S(1)} %reshape.220), channel_id=1, source_target_pairs={{0,1},{1,0},{2,3},{3,2},{4,5},{5,4},{6,7},{7,6},{8,9},{9,8},{10,11... | collective-permute-start | bytes 688136 | tf_op jit(solution)/shard_map/ppermute | solution.py:24
  71.4 17.8 %all-to-all-start.1 = ((bf16[4,128,896]{2,1,0:T(8,128)(2,1)}), bf16[4,128,896]{2,1,0:T(8,128)(2,1)S(1)}, u32[]{:S(2)}, u32[]{:S(2)}) async-start(bf16[4,128,896]{2,1,0:T(8,128)(2,1)} %bitcast.12), calls=%async_computation.1 | async-start | bytes 1835008 | tf_op jit(solution)/shard_map/all_to_all | solution.py:86
  75.5 9.1 %collective-permute-start.3 = (bf16[128,896]{1,0:T(8,128)(2,1)S(1)}, bf16[128,896]{1,0:T(8,128)(2,1)S(1)}, u32[]{:S(2)}, u32[]{:S(2)}) collective-permute-start(bf16[128,896]{1,0:T(8,128)(2,1)S(1)} %reshape.224), channel_id=1, source_target_pairs={{0,1},{1,0},{2,3},{3,2},{4,5},{5,4},{6,7},{7,6},{8,9},{9,8},{10,11... | collective-permute-start | bytes 688136 | tf_op jit(solution)/shard_map/ppermute | solution.py:24
  89.3 16.4 %all-to-all-start.4 = ((bf16[4,128,896]{2,1,0:T(8,128)(2,1)}), bf16[4,128,896]{2,1,0:T(8,128)(2,1)S(1)}, u32[]{:S(2)}, u32[]{:S(2)}) async-start(bf16[4,128,896]{2,1,0:T(8,128)(2,1)} %bitcast.17), calls=%async_computation.4 | async-start | bytes 1835008 | tf_op jit(solution)/shard_map/all_to_all | solution.py:86
  105.7 17.3 %all-to-all-start.2 = ((bf16[4,32,896]{2,1,0:T(8,128)(2,1)}), bf16[4,32,896]{2,1,0:T(8,128)(2,1)S(1)}, u32[]{:S(2)}, u32[]{:S(2)}) async-start(bf16[4,32,896]{2,1,0:T(8,128)(2,1)} %bitcast.13), calls=%async_computation.2 | async-start | bytes 458752 | tf_op jit(solution)/shard_map/all_to_all | solution.py:89
  123.0 15.1 %all-to-all-start.5 = ((bf16[4,32,896]{2,1,0:T(8,128)(2,1)}), bf16[4,32,896]{2,1,0:T(8,128)(2,1)S(1)}, u32[]{:S(2)}, u32[]{:S(2)}) async-start(bf16[4,32,896]{2,1,0:T(8,128)(2,1)} %bitcast.18), calls=%async_computation.5 | async-start | bytes 458752 | tf_op jit(solution)/shard_map/all_to_all | solution.py:89
  127.2 11.0 %copy-start.2 = (f32[1,32,3584]{2,1,0:T(8,128)S(1)}, f32[1,32,3584]{2,1,0:T(8,128)}, u32[]{:S(2)}) copy-start(f32[1,32,3584]{2,1,0:T(8,128)} %param.13) | copy-start | bytes 1376260
  127.2 11.0 %copy-start.3 = (bf16[1,32,3584]{2,1,0:T(8,128)(2,1)S(1)}, bf16[1,32,3584]{2,1,0:T(8,128)(2,1)}, u32[]{:S(2)}) copy-start(bf16[1,32,3584]{2,1,0:T(8,128)(2,1)} %param.15) | copy-start | bytes 688132
  127.2 11.0 %copy-start.4 = (bf16[1,32,3584]{2,1,0:T(8,128)(2,1)S(1)}, bf16[1,32,3584]{2,1,0:T(8,128)(2,1)}, u32[]{:S(2)}) copy-start(bf16[1,32,3584]{2,1,0:T(8,128)(2,1)} %param.14) | copy-start | bytes 688132

commit v2 on v0

v2 whole, which is shorter than its diff:
```python
import jax
import jax.numpy as jnp
from jax import lax
from jax.sharding import Mesh, PartitionSpec as P

AXES = ("y_hi", "x", "core", "z", "y_half", "y_low")
N_X = 4
TILE = 128

beta_one = 0.9
beta_two = 0.95
learn_rate = 0.00022
decay_rate = 0.1
epsilon = 1e-08
correct_one = 1.0 - 0.9**20
correct_two = 1.0 - 0.95**20


def contract_rows(left_rows, right_rows):
    return lax.dot_general(
        left_rows, right_rows, (((0,), (0,)), ((), ())), preferred_element_type=jnp.float32
    )


def on_device(
    hidden_acts, token_gradients, local_hidden, local_grads, counts, weight, moment, second
):
    x = lax.axis_index("x")
    core = lax.axis_index("core")
    expert_id = lax.axis_index("z") * 2 + lax.axis_index("y_half")
    outgoing = token_gradients[0, 0]
    slots, features = outgoing.shape[1:]
    hidden = hidden_acts[0, 0]
    rows, units = hidden.shape
    span = features // N_X
    width = (span // TILE + 1) // 2 * TILE
    shift = span - width

    arrived = lax.all_to_all(outgoing, ("z", "y_half"), 0, 0, tiled=True)

    filled = lax.dynamic_index_in_dim(counts[0], expert_id, axis=1, keepdims=False)
    slot_ids = jnp.arange(slots, dtype=jnp.int32)
    is_live = (slot_ids[None, :] < filled[:, None]).reshape(rows)
    hidden = jnp.where(is_live[:, None], hidden, jnp.zeros_like(hidden))
    hidden = hidden.reshape(-1, 2, slots, units).transpose(1, 0, 2, 3).reshape(rows, units)
    owned_hidden = local_hidden[0, 0]
    owned_gradients = local_grads[0, 0]

    held = []
    for step in range(N_X):
        start = lax.rem(x + step, N_X) * span
        block = lax.dynamic_slice_in_dim(owned_gradients, start, span, axis=1)
        block = jnp.concatenate([block, hidden, owned_hidden], axis=1)
        if step:
            block = lax.ppermute(block, "x", [(i, (i + step) % N_X) for i in range(N_X)])
        held.append(block)
    held = jnp.stack(held)
    mine = lax.dynamic_slice_in_dim(held[:, :, :span], core * shift, width, axis=2)
    other = lax.dynamic_slice_in_dim(held[:, :, :span], (1 - core) * shift, width, axis=2)
    other = jnp.concatenate([other, held[:, :, span:]], axis=2)
    other = lax.ppermute(other, "core", [(0, 1), (1, 0)])
    left = jnp.concatenate(
        [held[:, :, span + units :].reshape(-1, units), other[:, :, width + units :].reshape(-1, units)]
    )
    right = jnp.concatenate(
        [mine.reshape(-1, width), other[:, :, :width].reshape(-1, width)]
    )
    partial = contract_rows(left, right)

    own = held[:, :, span : span + units]
    far = other[:, :, width : width + units]
    pair = jnp.stack([jnp.where(core == 0, own, far), jnp.where(core == 0, far, own)], axis=1)
    back = jnp.flip(pair, 0)
    twice = jnp.concatenate([back, back])
    routed = lax.dynamic_slice_in_dim(twice, N_X - 1 - x, N_X, axis=0).reshape(-1, units)

    near = arrived.reshape(-1, features)
    blocks = jnp.stack(
        [
            near[:, i * span + j * shift : i * span + j * shift + width]
            for i in range(N_X)
            for j in range(2)
            for _ in range(2)
        ]
    )
    gathered = lax.all_to_all(blocks, ("x", "core", "y_low"), 0, 0, tiled=True)
    partial = partial + contract_rows(routed, gathered.reshape(-1, width))

    partial = partial.astype(jnp.bfloat16).reshape(4 * N_X, -1, width)
    partial = lax.all_to_all(partial, ("y_hi", "x", "core"), 0, 0, tiled=True)
    partial = partial.astype(jnp.float32).reshape(2, N_X, 2, -1, width)
    summed = partial[0] + partial[1]
    summed = jnp.concatenate(
        [
            part
            for i in range(N_X)
            for part in (summed[i, 0], summed[i, 1][:, 2 * width - span :])
        ],
        axis=1,
    )
    moment_new = beta_one * moment[0].astype(jnp.float32) + (1.0 - beta_one) * summed
    second_new = beta_two * second[0].astype(jnp.float32) + (1.0 - beta_two) * summed * summed
    step_direction = moment_new / correct_one / (jnp.sqrt(second_new / correct_two) + epsilon)
    master = weight[0]
    new_weight = master - learn_rate * (step_direction + decay_rate * master)
    return (
        new_weight[None],
        moment_new.astype(jnp.bfloat16)[None],
        second_new.astype(jnp.bfloat16)[None],
    )


def solution(mesh):
    dp = ("y_hi", "x", "core")
    expert = ("z", "y_half", "y_low")
    fine = Mesh(mesh.devices.reshape(2, N_X, 2, 16, 2, 2), AXES)
    outs = P(expert, dp, None)
    return jax.shard_map(
        on_device,
        mesh=fine,
        in_specs=(
            P(dp, expert, None, None),
            P(dp, expert, None, None, None),
            P(dp, expert, None, None),
            P(dp, expert, None, None),
            P(dp, None, None),
            outs,
            outs,
            outs,
        ),
        out_specs=(outs, outs, outs),
        check_vma=False,
    )
```

time: 211 us -> 123 us (0.58)
  the two profiles are of different devices: /device:TPU:8 before, /device:TPU:16 now
where the time goes in v2:
time: 123 us; the launch traced here: 122 us
  starting transfers between devices  37.2 us (30%)
  waiting for transfers between devices  32.3 us (26%)
  blocking collectives  27.4 us (22%)
  local copies, waits for them, and re-layouts  14.3 us (12%)
  other arithmetic  8.78 us (7%)
  matrix products  1.46 us (1%)
    all_to_all x1, blocking collectives, on_device(): partial = lax.all_to_all(partial, ('y_hi', 'x', 'core'), 0, 0, tiled=True)  27.4 us
    all_to_all x1, starting transfers between devices, on_device(): arrived = lax.all_to_all(outgoing, ('z', 'y_half'), 0, 0, tiled=True)  21.4 us
    ppermute x3, waiting for transfers between devices, on_device(): lax.ppermute(block, 'x', [(i, (i + step) % N_X) for i in range(N_X)])  20.6 us
    all_to_all x1, waiting for transfers between devices, on_device(): gathered = lax.all_to_all(blocks, ('x', 'core', 'y_low'), 0, 0, tiled=True)  11.7 us
    unnamed x42, local copies, waits for them, and re-layouts  11 us
    ppermute x3, starting transfers between devices, on_device(): lax.ppermute(block, 'x', [(i, (i + step) % N_X) for i in range(N_X)])  10.2 us
    all_to_all x1, starting transfers between devices, on_device(): gathered = lax.all_to_all(blocks, ('x', 'core', 'y_low'), 0, 0, tiled=True)  3.65 us
    another operation x2, other arithmetic, on_device(): jnp.stack([jnp.where(core == 0, own, far), jnp.where(core == 0, far, own)...  2.66 us
  transfers between devices with their start and end apart: 6, of which 3 were waited for; matrix products, arithmetic and copies ran while one was open for 16% of the time, Pallas kernels for 0%

profile of v2, /device:TPU:16, one launch (start us, length us, event | category | flops | bytes accessed | tf_op | source)
XLA Modules:
  0.0 122.4 jit_solution(4417839999440512059)
XLA Ops:
  0.7 21.4 %all-to-all-start = ((bf16[32,2,3584]{2,1,0:T(2,128)(2,1)}), bf16[32,2,3584]{2,1,0:T(2,128)(2,1)S(1)}, u32[]{:S(2)}, u32[]{:S(2)}) async-start(bf16[32,2,3584]{2,1,0:T(2,128)(2,1)} %bitcast.135), calls=%async_computation | async-start | bytes 917504 | tf_op jit(solution)/shard_map/all_to_all | solution.py:39
  22.4 1.0 squeeze.16
  23.8 1.0 fusion.8
  24.8 4.7 %collective-permute-start.2 = (bf16[128,1920]{1,0:T(8,128)(2,1)}, bf16[128,1920]{1,0:T(8,128)(2,1)}, u32[]{:S(2)}, u32[]{:S(2)}) collective-permute-start(bf16[128,1920]{1,0:T(8,128)(2,1)} %get-tuple-element.24), channel_id=1, source_target_pairs={{0,384},{128,0},{256,128},{384,256},{1,385},{129,1},{257,129},{385... | collective-permute-start | bytes 1474568 | tf_op jit(solution)/shard_map/ppermute | solution.py:55
  29.4 2.7 %collective-permute-start.1 = (bf16[128,1920]{1,0:T(8,128)(2,1)S(1)}, bf16[128,1920]{1,0:T(8,128)(2,1)}, u32[]{:S(2)}, u32[]{:S(2)}) collective-permute-start(bf16[128,1920]{1,0:T(8,128)(2,1)S(1)} %get-tuple-element.23), channel_id=1, source_target_pairs={{0,256},{128,384},{256,0},{384,128},{1,257},{129,385},{257,1},{385... | collective-permute-start | bytes 1474568 | tf_op jit(solution)/shard_map/ppermute | solution.py:55
  32.1 2.8 %collective-permute-start = (bf16[128,1920]{1,0:T(8,128)(2,1)S(1)}, bf16[128,1920]{1,0:T(8,128)(2,1)}, u32[]{:S(2)}, u32[]{:S(2)}) collective-permute-start(bf16[128,1920]{1,0:T(8,128)(2,1)S(1)} %get-tuple-element.22), channel_id=1, source_target_pairs={{0,128},{128,256},{256,384},{384,0},{1,129},{129,257},{257,385},{3... | collective-permute-start | bytes 1474568 | tf_op jit(solution)/shard_map/ppermute | solution.py:55
  35.0 15.3 %collective-permute-done.2 = bf16[128,1920]{1,0:T(8,128)(2,1)} collective-permute-done((bf16[128,1920]{1,0:T(8,128)(2,1)}, bf16[128,1920]{1,0:T(8,128)(2,1)}, u32[]{:S(2)}, u32[]{:S(2)}) %collective-permute-start.2) | collective-permute-done | bytes 491552 | tf_op jit(solution)/shard_map/ppermute | solution.py:55
  50.2 5.4 %collective-permute-done = bf16[128,1920]{1,0:T(8,128)(2,1)} collective-permute-done((bf16[128,1920]{1,0:T(8,128)(2,1)S(1)}, bf16[128,1920]{1,0:T(8,128)(2,1)}, u32[]{:S(2)}, u32[]{:S(2)}) %collective-permute-start) | collective-permute-done | bytes 491552 | tf_op jit(solution)/shard_map/ppermute | solution.py:55
  55.6 1.6 %pad_maximum_fusion = bf16[4,128,1920]{2,1,0:T(8,128)(2,1)S(1)} fusion(bf16[1,128,1920]{2,1,0:T(8,128)(2,1)} %bitcast.9, bf16[1,128,1920]{2,1,0:T(8,128)(2,1)} %bitcast.7, bf16[1,128,1920]{2,1,0:T(8,128)(2,1)} %bitcast.5, bf16[1,128,1920]{2,1,0:T(8,128)(2,1)S(1)} %get-tuple-element.21), kind=kLoop, calls=%fused_computation.2 | loop fusion | flops 2949120 | bytes 3932160 | tf_op jit(solution)/shard_map/stack | solution.py:57
  57.4 0.9 constant_dynamic-slice_fusion
  58.3 1.2 %pad_maximum_fusion.1 = bf16[4,128,1536]{2,1,0:T(8,128)(2,1)} fusion(bf16[4,128,1024]{2,1,0:T(8,128)(2,1)S(1)} %slice.129, bf16[4,128,512]{2,1,0:T(8,128)(2,1)S(1)} %get-tuple-element.9), kind=kLoop, calls=%fused_computation.3 | loop fusion | flops 3145728 | bytes 3145728 | tf_op jit(solution)/shard_map/concatenate | solution.py:60
  59.6 1.9 %collective-permute-start.3 = (bf16[4,128,1536]{2,1,0:T(8,128)(2,1)}, bf16[4,128,1536]{2,1,0:T(8,128)(2,1)}, u32[]{:S(2)}, u32[]{:S(2)}) collective-permute-start(bf16[4,128,1536]{2,1,0:T(8,128)(2,1)} %pad_maximum_fusion.1), channel_id=1, source_target_pairs={{0,64},{64,0},{1,65},{65,1},{2,66},{66,2},{3,67},{67,3},{4,68},{68... | collective-permute-start | bytes 4718600 | tf_op jit(solution)/shard_map/ppermute | solution.py:61
  63.5 0.6 constant_dynamic-update-slice_fusion.12
  65.4 0.6 constant_dynamic-update-slice_fusion.9
  66.7 0.6 constant_dynamic-update-slice_fusion.7
  68.5 0.6 constant_dynamic-update-slice_fusion.4
  71.7 3.7 %all-to-all-start.1 = ((bf16[16,64,512]{2,1,0:T(8,128)(2,1)}), bf16[16,64,512]{2,1,0:T(8,128)(2,1)S(1)}, u32[]{:S(2)}, u32[]{:S(2)}) async-start(bf16[16,64,512]{2,1,0:T(8,128)(2,1)} %constant_dynamic-update-slice_fusion), calls=%async_computation.1 | async-start | bytes 2097152 | tf_op jit(solution)/shard_map/all_to_all | solution.py:86
  75.3 2.6 %select_bitcast_fusion.1 = (bf16[4,1,128,512]{3,2,1,0:T(8,128)(2,1)S(1)}, bf16[4,1,128,512]{3,2,1,0:T(8,128)(2,1)S(1)}, bf16[4,128,512]{2,1,0:T(8,128)(2,1)}, bf...) fusion(pred[]{:T(512)S(6)} %eq.4, bf16[4,128,1536]{2,1,0:T(8,128)(2,1)} %collective-permute-done.3, ...), kind=kLoop, calls=%fused_computation.25 | loop fusion | flops 524288 | bytes 5242881 | tf_op jit(solution)/shard_map/stack | solution.py:72
  78.5 11.7 %all-to-all-done.1 = bf16[16,64,512]{2,1,0:T(8,128)(2,1)S(1)} async-done(((bf16[16,64,512]{2,1,0:T(8,128)(2,1)}), bf16[16,64,512]{2,1,0:T(8,128)(2,1)S(1)}, u32[]{:S(2)}, u32[]{:S(2)}) %all-to-all-start.1) | async-done | bytes 1048608 | tf_op jit(solution)/shard_map/all_to_all | solution.py:86
  90.2 0.7 fusion.19
  91.7 0.7 fusion
  92.4 27.4 %all_to_all.15 = bf16[16,32,512]{2,1,0:T(8,128)(2,1)S(1)} all-to-all(bf16[16,32,512]{2,1,0:T(8,128)(2,1)S(1)} %bitcast.130), channel_id=1, replica_groups=mesh['y_hi'=2,'x'=4,'core'=2,'z'=16,'y_half'=2,'y_low'=2] {'y_hi','x','c..., dimensions={0} | all-to-all | bytes 1048576 | tf_op jit(solution)/shard_map/all_to_all | solution.py:90
  120.2 0.7 copy-done.6
  121.0 1.4 %fusion.11 = (bf16[1,32,3584]{2,1,0:T(8,128)(2,1)}, f32[1,32,3584]{2,1,0:T(8,128)}, bf16[1,32,3584]{2,1,0:T(8,128)(2,1)}) fusion(f32[1,32,3584]{2,1,0:T(8,128)S(1)} %constant_dynamic-update-slice_fusion.16, bf16[1,32,3584]{2,1,0:T(8,128)(2,1)S(1)} %copy-done.7, f32[1,32,3584]{2,1,0:T(8,128)S(1)} %copy-done.6, bf16[1,32,3584]{2,1,0:T(8,128)(2,1)S(1)} %copy-done.8), kind=kLoop, calls=%fused_computation.32 | loop fusion | flops 2179072 | bytes 2293760 | tf_op jit(solution)/shard_map/convert_element_type | solution.py:109
  (58 shorter events, 10.3 us)
Async XLA Ops:
  0.6 21.5 %copy-start = (s32[1,64,32]{1,2,0:T(8,128)S(1)}, s32[1,64,32]{1,2,0:T(8,128)}, u32[]{:S(2)}) copy-start(s32[1,64,32]{1,2,0:T(8,128)} %param.12) | copy-start | bytes 24580
  0.6 23.0 %copy-start.1 = (bf16[1,1,128,3584]{3,2,1,0:T(8,128)(2,1)S(1)}, bf16[1,1,128,3584]{3,2,1,0:T(8,128)(2,1)}, u32[]{:S(2)}) copy-start(bf16[1,1,128,3584]{3,2,1,0:T(8,128)(2,1)} %param.11) | copy-start | bytes 2752516
  0.7 23.1 %copy-start.9 = (bf16[1,1,128,512]{3,2,1,0:T(8,128)(2,1)S(1)}, bf16[1,1,128,512]{3,2,1,0:T(8,128)(2,1)}, u32[]{:S(2)}) copy-start(bf16[1,1,128,512]{3,2,1,0:T(8,128)(2,1)} %param.10) | copy-start | bytes 393220
  0.7 60.8 %all-to-all-start = ((bf16[32,2,3584]{2,1,0:T(2,128)(2,1)}), bf16[32,2,3584]{2,1,0:T(2,128)(2,1)S(1)}, u32[]{:S(2)}, u32[]{:S(2)}) async-start(bf16[32,2,3584]{2,1,0:T(2,128)(2,1)} %bitcast.135), calls=%async_computation | async-start | bytes 917504 | tf_op jit(solution)/shard_map/all_to_all | solution.py:39
  24.8 25.4 %collective-permute-start.2 = (bf16[128,1920]{1,0:T(8,128)(2,1)}, bf16[128,1920]{1,0:T(8,128)(2,1)}, u32[]{:S(2)}, u32[]{:S(2)}) collective-permute-start(bf16[128,1920]{1,0:T(8,128)(2,1)} %get-tuple-element.24), channel_id=1, source_target_pairs={{0,384},{128,0},{256,128},{384,256},{1,385},{129,1},{257,129},{385... | collective-permute-start | bytes 1474568 | tf_op jit(solution)/shard_map/ppermute | solution.py:55
  29.4 20.8 %collective-permute-start.1 = (bf16[128,1920]{1,0:T(8,128)(2,1)S(1)}, bf16[128,1920]{1,0:T(8,128)(2,1)}, u32[]{:S(2)}, u32[]{:S(2)}) collective-permute-start(bf16[128,1920]{1,0:T(8,128)(2,1)S(1)} %get-tuple-element.23), channel_id=1, source_target_pairs={{0,256},{128,384},{256,0},{384,128},{1,257},{129,385},{257,1},{385... | collective-permute-start | bytes 1474568 | tf_op jit(solution)/shard_map/ppermute | solution.py:55
  32.1 23.4 %collective-permute-start = (bf16[128,1920]{1,0:T(8,128)(2,1)S(1)}, bf16[128,1920]{1,0:T(8,128)(2,1)}, u32[]{:S(2)}, u32[]{:S(2)}) collective-permute-start(bf16[128,1920]{1,0:T(8,128)(2,1)S(1)} %get-tuple-element.22), channel_id=1, source_target_pairs={{0,128},{128,256},{256,384},{384,0},{1,129},{129,257},{257,385},{3... | collective-permute-start | bytes 1474568 | tf_op jit(solution)/shard_map/ppermute | solution.py:55
  59.6 15.8 %collective-permute-start.3 = (bf16[4,128,1536]{2,1,0:T(8,128)(2,1)}, bf16[4,128,1536]{2,1,0:T(8,128)(2,1)}, u32[]{:S(2)}, u32[]{:S(2)}) collective-permute-start(bf16[4,128,1536]{2,1,0:T(8,128)(2,1)} %pad_maximum_fusion.1), channel_id=1, source_target_pairs={{0,64},{64,0},{1,65},{65,1},{2,66},{66,2},{3,67},{67,3},{4,68},{68... | collective-permute-start | bytes 4718600 | tf_op jit(solution)/shard_map/ppermute | solution.py:61
  71.7 18.5 %all-to-all-start.1 = ((bf16[16,64,512]{2,1,0:T(8,128)(2,1)}), bf16[16,64,512]{2,1,0:T(8,128)(2,1)S(1)}, u32[]{:S(2)}, u32[]{:S(2)}) async-start(bf16[16,64,512]{2,1,0:T(8,128)(2,1)} %constant_dynamic-update-slice_fusion), calls=%async_computation.1 | async-start | bytes 2097152 | tf_op jit(solution)/shard_map/all_to_all | solution.py:86
  90.2 1.0 copy-start.2
  90.2 1.2 copy-start.3
  90.2 1.4 %copy-start.4 = (bf16[4,128,512]{2,1,0:T(8,128)(2,1)S(1)}, bf16[4,128,512]{2,1,0:T(8,128)(2,1)}, u32[]{:S(2)}) copy-start(bf16[4,128,512]{2,1,0:T(8,128)(2,1)} %get-tuple-element.6) | copy-start | bytes 1572868
  90.2 1.5 %copy-start.5 = (bf16[4,128,512]{2,1,0:T(8,128)(2,1)S(1)}, bf16[4,128,512]{2,1,0:T(8,128)(2,1)}, u32[]{:S(2)}) copy-start(bf16[4,128,512]{2,1,0:T(8,128)(2,1)} %get-tuple-element.7) | copy-start | bytes 1572868
  119.8 1.0 copy-start.6
  119.8 1.1 copy-start.7
  119.8 1.2 copy-start.8

commit v3 on v2

v3 whole, which is shorter than its diff:
```python
import jax
import jax.numpy as jnp
from jax import lax
from jax.experimental import pallas as pl
from jax.experimental.pallas import tpu as pltpu
from jax.sharding import Mesh, PartitionSpec as P

AXES = ("y_hi", "x", "core", "z", "y_half", "y_low")
N_X = 4
TILE = 128

beta_one = 0.9
beta_two = 0.95
learn_rate = 0.00022
decay_rate = 0.1
epsilon = 1e-08
correct_one = 1.0 - 0.9**20
correct_two = 1.0 - 0.95**20


def contract_rows(left_rows, right_rows):
    return lax.dot_general(
        left_rows, right_rows, (((0,), (0,)), ((), ())), preferred_element_type=jnp.float32
    )


def column_blocks(near, span):
    rows = near.shape[0]

    def kernel(near_ref, out_ref):
        for i in range(N_X):
            block = near_ref[:, i * span : (i + 1) * span]
            for j in range(2):
                out_ref[2 * i + j] = block

    return pl.pallas_call(
        kernel,
        out_shape=jax.ShapeDtypeStruct((2 * N_X, rows, span), near.dtype),
        in_specs=[pl.BlockSpec(memory_space=pltpu.VMEM)],
        out_specs=pl.BlockSpec(memory_space=pltpu.VMEM),
    )(near)


def adamw(sums, weight, moment, second):
    rows, features = weight.shape[1:]
    width = sums.shape[-1]
    span = features // N_X

    def kernel(sums_ref, weight_ref, moment_ref, second_ref, new_weight, new_moment, new_second):
        for j in range(2):
            skip = j * (2 * width - span)
            cols = slice(j * width, j * width + width - skip)
            summed = sums_ref[0, 0, j, :, skip:].astype(jnp.float32)
            summed = summed + sums_ref[1, 0, j, :, skip:].astype(jnp.float32)
            first = beta_one * moment_ref[0, :, cols].astype(jnp.float32)
            first = first + (1.0 - beta_one) * summed
            next_ = beta_two * second_ref[0, :, cols].astype(jnp.float32)
            next_ = next_ + (1.0 - beta_two) * summed * summed
            direction = first / correct_one / (jnp.sqrt(next_ / correct_two) + epsilon)
            master = weight_ref[0, :, cols]
            new_weight[0, :, cols] = master - learn_rate * (direction + decay_rate * master)
            new_moment[0, :, cols] = first.astype(jnp.bfloat16)
            new_second[0, :, cols] = next_.astype(jnp.bfloat16)

    shard = pl.BlockSpec((1, rows, span), lambda i: (0, 0, i))
    return pl.pallas_call(
        kernel,
        grid=(N_X,),
        out_shape=tuple(jax.ShapeDtypeStruct(a.shape, a.dtype) for a in (weight, moment, second)),
        in_specs=[
            pl.BlockSpec((2, 1, 2, rows, width), lambda i: (0, i, 0, 0, 0)),
            shard,
            shard,
            shard,
        ],
        out_specs=(shard, shard, shard),
    )(sums, weight, moment, second)


def on_device(
    hidden_acts, token_gradients, local_hidden, local_grads, counts, weight, moment, second
):
    x = lax.axis_index("x")
    core = lax.axis_index("core")
    expert_id = lax.axis_index("z") * 2 + lax.axis_index("y_half")
    outgoing = token_gradients[0, 0]
    slots, features = outgoing.shape[1:]
    hidden = hidden_acts[0, 0]
    rows, units = hidden.shape
    span = features // N_X
    width = (span // TILE + 1) // 2 * TILE
    shift = span - width

    arrived = lax.all_to_all(outgoing, ("z", "y_half"), 0, 0, tiled=True)

    filled = lax.dynamic_index_in_dim(counts[0], expert_id, axis=1, keepdims=False)
    slot_ids = jnp.arange(slots, dtype=jnp.int32)
    is_live = (slot_ids[None, :] < filled[:, None]).reshape(rows)
    hidden = jnp.where(is_live[:, None], hidden, jnp.zeros_like(hidden))
    hidden = hidden.reshape(-1, 2, slots, units).transpose(1, 0, 2, 3).reshape(rows, units)
    owned_hidden = local_hidden[0, 0]
    owned_gradients = local_grads[0, 0]

    held = []
    for step in range(N_X):
        start = lax.rem(x + step, N_X) * span
        block = lax.dynamic_slice_in_dim(owned_gradients, start, span, axis=1)
        held.append(jnp.concatenate([block, hidden, owned_hidden], axis=1))
    for step in (2, 1, 3):
        held[step] = lax.ppermute(
            held[step], "x", [(i, (i + step) % N_X) for i in range(N_X)]
        )

    blocks = column_blocks(arrived.reshape(-1, features), span)
    held, _ = lax.optimization_barrier((held, blocks))
    gathered = lax.all_to_all(blocks, ("x", "y_low"), 0, 0, tiled=True)
    gathered = gathered.reshape(-1, span)

    back = jnp.stack([block[:, span : span + units] for block in held[::-1]])
    twice = jnp.concatenate([back, back])
    routed = lax.dynamic_slice_in_dim(twice, N_X - 1 - x, N_X, axis=0).reshape(-1, units)
    owned = jnp.concatenate([block[:, span + units :] for block in held])
    columns = jnp.concatenate([block[:, :span] for block in held])

    def partial_of(which):
        start = which * shift
        return contract_rows(
            owned, lax.dynamic_slice_in_dim(columns, start, width, axis=1)
        ) + contract_rows(routed, lax.dynamic_slice_in_dim(gathered, start, width, axis=1))

    other = partial_of(1 - core).astype(jnp.bfloat16)
    other = lax.ppermute(other, "core", [(0, 1), (1, 0)])
    partial = partial_of(core) + other.astype(jnp.float32)

    partial = partial.astype(jnp.bfloat16).reshape(4 * N_X, -1, width)
    partial = lax.all_to_all(partial, ("y_hi", "x", "core"), 0, 0, tiled=True)
    return adamw(partial.reshape(2, N_X, 2, -1, width), weight, moment, second)


def solution(mesh):
    dp = ("y_hi", "x", "core")
    expert = ("z", "y_half", "y_low")
    fine = Mesh(mesh.devices.reshape(2, N_X, 2, 16, 2, 2), AXES)
    outs = P(expert, dp, None)
    return jax.shard_map(
        on_device,
        mesh=fine,
        in_specs=(
            P(dp, expert, None, None),
            P(dp, expert, None, None, None),
            P(dp, expert, None, None),
            P(dp, expert, None, None),
            P(dp, None, None),
            outs,
            outs,
            outs,
        ),
        out_specs=(outs, outs, outs),
        check_vma=False,
    )
```

time: 123 us -> 108 us (0.88)
  local copies, waits for them, and re-layouts: 14.3 us -> 4.11 us
  other arithmetic: 8.78 us -> 1.51 us
  waiting for transfers between devices: 32.3 us -> 26.4 us
  Pallas kernels: 0 us -> 5.57 us
  matrix products: 1.46 us -> 3.7 us
  starting transfers between devices: 37.2 us -> 39.4 us
  blocking collectives: 27.4 us -> 25.5 us
    ppermute x3, waiting for transfers between devices: 20.6 us -> 0.01 us  [on_device(): lax.ppermute(held[step], 'x', [(i, (i + step) % N_X) for i in range(N_X)])]
    all_to_all x1, waiting for transfers between devices: 0.01 us -> 16.4 us  [on_device(): arrived = lax.all_to_all(outgoing, ('z', 'y_half'), 0, 0, tiled=True)]
    unnamed x42 -> x27, local copies, waits for them, and re-layouts: 11 us -> 1.66 us
    pallas_call x0 -> x2, Pallas kernels: none -> 5.57 us  [the longest x1 3.55 us: adamw(): pl.pallas_call(kernel, grid=(N_X,), out_shape=tuple((jax.ShapeDtypeStruct...]
    another operation x4 -> x0, other arithmetic: 5.24 us -> none  [the longest x2 2.66 us: on_device(): jnp.stack([jnp.where(core == 0, own, far), jnp.where(core == 0, far, own)...]
    all_to_all x1, waiting for transfers between devices: 11.7 us -> 9.36 us  [on_device(): gathered = lax.all_to_all(blocks, ('x', 'y_low'), 0, 0, tiled=True)]
    dot_general x2 -> x4, matrix products: 1.46 us -> 3.7 us  [contract_rows(): lax.dot_general(left_rows, right_rows, (((0,), (0,)), ((), ())), preferre...]
    all_to_all x1, blocking collectives: 27.4 us -> 25.5 us  [on_device(): partial = lax.all_to_all(partial, ('y_hi', 'x', 'core'), 0, 0, tiled=True)]
  transfers between devices with their start and end apart: 6 -> 6, of which waited for: 3 -> 3; matrix products, arithmetic and copies ran while one was open for 16% -> 5% of each run, Pallas kernels for 0% -> 2%
where the time goes in v3:
time: 108 us; the launch traced here: 107 us
  starting transfers between devices  39.4 us (36%)
  waiting for transfers between devices  26.4 us (24%)
  blocking collectives  25.5 us (24%)
  Pallas kernels  5.57 us (5%)
  local copies, waits for them, and re-layouts  4.11 us (4%)
  matrix products  3.7 us (3%)
  other arithmetic  1.51 us (1%)
    all_to_all x1, blocking collectives, on_device(): partial = lax.all_to_all(partial, ('y_hi', 'x', 'core'), 0, 0, tiled=True)  25.5 us
    all_to_all x1, starting transfers between devices, on_device(): arrived = lax.all_to_all(outgoing, ('z', 'y_half'), 0, 0, tiled=True)  21.4 us
    all_to_all x1, waiting for transfers between devices, on_device(): arrived = lax.all_to_all(outgoing, ('z', 'y_half'), 0, 0, tiled=True)  16.4 us
    ppermute x3, starting transfers between devices, on_device(): lax.ppermute(held[step], 'x', [(i, (i + step) % N_X) for i in range(N_X)])  10.8 us
    all_to_all x1, waiting for transfers between devices, on_device(): gathered = lax.all_to_all(blocks, ('x', 'y_low'), 0, 0, tiled=True)  9.36 us
    all_to_all x1, starting transfers between devices, on_device(): gathered = lax.all_to_all(blocks, ('x', 'y_low'), 0, 0, tiled=True)  5.31 us
    dot_general x4, matrix products, contract_rows(): lax.dot_general(left_rows, right_rows, (((0,), (0,)), ((), ())), preferre...  3.7 us
    pallas_call x1, Pallas kernels, adamw(): pl.pallas_call(kernel, grid=(N_X,), out_shape=tuple((jax.ShapeDtypeStruct...  3.55 us
  transfers between devices with their start and end apart: 6, of which 3 were waited for; matrix products, arithmetic and copies ran while one was open for 5% of the time, Pallas kernels for 2%

profile of v3, /device:TPU:16, one launch (start us, length us, event | category | flops | bytes accessed | tf_op | source)
XLA Modules:
  0.0 107.3 jit_solution(9902961697339936701)
XLA Ops:
  0.7 21.4 %all-to-all-start = ((bf16[32,2,3584]{2,1,0:T(2,128)(2,1)}), bf16[32,2,3584]{2,1,0:T(2,128)(2,1)S(1)}, u32[]{:S(2)}, u32[]{:S(2)}) async-start(bf16[32,2,3584]{2,1,0:T(2,128)(2,1)} %bitcast.38), calls=%async_computation | async-start | bytes 917504 | tf_op jit(solution)/shard_map/all_to_all | solution.py:94
  22.4 0.2 fusion.9
  22.9 0.7 copy-done.5
  23.7 1.1 %pad_maximum_fusion.1 = (bf16[128,1920]{1,0:T(8,128)(2,1)}, bf16[128,1920]{1,0:T(8,128)(2,1)}, bf16[128,1920]{1,0:T(8,128)(2,1)S(1)}, bf16[128,1920]{1,0:T(8,128)(2,1)S(1)}) fusion(bf16[128,512]{1,0:T(8,128)(2,1)S(1)} %bitcast.39, bf16[128,512]{1,0:T(8,128)(2,1)S(1)} %reshape.55, bf16[128,896]{1,0:T(8,128)(2,1)S(1)} %get-tuple-element.11, ...), kind=kLoop, calls=%fused_computation.5 | loop fusion | flops 4423680 | bytes 3145728 | tf_op jit(solution)/shard_map/concatenate | solution.py:108
  24.8 4.7 %collective-permute-start.2 = (bf16[128,1920]{1,0:T(8,128)(2,1)}, bf16[128,1920]{1,0:T(8,128)(2,1)S(1)}, u32[]{:S(2)}, u32[]{:S(2)}) collective-permute-start(bf16[128,1920]{1,0:T(8,128)(2,1)} %get-tuple-element.15), channel_id=1, source_target_pairs={{0,384},{128,0},{256,128},{384,256},{1,385},{129,1},{257,129},{385... | collective-permute-start | bytes 1474568 | tf_op jit(solution)/shard_map/ppermute | solution.py:110
  29.5 1.9 %collective-permute-start = (bf16[128,1920]{1,0:T(8,128)(2,1)}, bf16[128,1920]{1,0:T(8,128)(2,1)S(1)}, u32[]{:S(2)}, u32[]{:S(2)}) collective-permute-start(bf16[128,1920]{1,0:T(8,128)(2,1)} %get-tuple-element.16), channel_id=1, source_target_pairs={{0,128},{128,256},{256,384},{384,0},{1,129},{129,257},{257,385},{3... | collective-permute-start | bytes 1474568 | tf_op jit(solution)/shard_map/ppermute | solution.py:110
  31.4 4.2 %collective-permute-start.1 = (bf16[128,1920]{1,0:T(8,128)(2,1)S(1)}, bf16[128,1920]{1,0:T(8,128)(2,1)S(1)}, u32[]{:S(2)}, u32[]{:S(2)}) collective-permute-start(bf16[128,1920]{1,0:T(8,128)(2,1)S(1)} %get-tuple-element.17), channel_id=1, source_target_pairs={{0,256},{128,384},{256,0},{384,128},{1,257},{129,385},{257,1},{385... | collective-permute-start | bytes 1474568 | tf_op jit(solution)/shard_map/ppermute | solution.py:110
  35.6 16.4 %all-to-all-done = bf16[32,2,3584]{2,1,0:T(2,128)(2,1)S(1)} async-done(((bf16[32,2,3584]{2,1,0:T(2,128)(2,1)}), bf16[32,2,3584]{2,1,0:T(2,128)(2,1)S(1)}, u32[]{:S(2)}, u32[]{:S(2)}) %all-to-all-start) | async-done | bytes 458784 | tf_op jit(solution)/shard_map/all_to_all | solution.py:94
  52.0 0.9 reshape.56.near_ref
  52.9 2.0 %shard_map.103 = bf16[8,64,896]{2,1,0:T(8,128)(2,1)} custom-call(bf16[64,3584]{1,0:T(8,128)(2,1)} %reshape.56.near_ref), custom_call_target="tpu_custom_call" | custom-call | tf_op jit(solution)/shard_map/pallas_call | solution.py:36
  55.0 5.3 %all-to-all-start.1 = ((bf16[8,64,896]{2,1,0:T(8,128)(2,1)}), bf16[8,64,896]{2,1,0:T(8,128)(2,1)S(1)}, u32[]{:S(2)}, u32[]{:S(2)}) async-start(bf16[8,64,896]{2,1,0:T(8,128)(2,1)} %shard_map.103), calls=%async_computation.1 | async-start | bytes 1835008 | tf_op jit(solution)/shard_map/all_to_all | solution.py:116
  60.6 0.7 copy-done.3
  61.3 0.1 copy-done.1
  61.5 0.7 slice-done.2
  62.2 0.2 slice-done.1
  62.6 0.5 fusion.2
  63.1 9.4 %all-to-all-done.1 = bf16[8,64,896]{2,1,0:T(8,128)(2,1)S(1)} async-done(((bf16[8,64,896]{2,1,0:T(8,128)(2,1)}), bf16[8,64,896]{2,1,0:T(8,128)(2,1)S(1)}, u32[]{:S(2)}, u32[]{:S(2)}) %all-to-all-start.1) | async-done | bytes 917536 | tf_op jit(solution)/shard_map/all_to_all | solution.py:116
  72.4 1.3 %fusion = bf16[512,512]{1,0:T(8,128)(2,1)} fusion(f32[512,512]{1,0:T(8,128)S(1)} %fusion.2, bf16[512,512]{1,0:T(8,128)(2,1)S(1)} %bitcast.32, bf16[512,896]{1,0:T(8,128)(2,1)S(1)} %bitcast.34, s32[]{:T(128)S(6)} %select_n.40), kind=kOutput, calls=%fused_computation.2 | convolution fusion | flops 268959744 | bytes 2621444 | tf_op jit(solution)/shard_map/dot_general | solution.py:22
  73.7 1.9 %collective-permute-start.3 = (bf16[512,512]{1,0:T(8,128)(2,1)}, bf16[512,512]{1,0:T(8,128)(2,1)S(1)}, u32[]{:S(2)}, u32[]{:S(2)}) collective-permute-start(bf16[512,512]{1,0:T(8,128)(2,1)} %fusion), channel_id=1, source_target_pairs={{0,64},{64,0},{1,65},{65,1},{2,66},{66,2},{3,67},{67,3},{4,68},{68... | collective-permute-start | bytes 1572872 | tf_op jit(solution)/shard_map/ppermute | solution.py:132
  75.6 1.5 %fusion.7 = f32[512,512]{1,0:T(8,128)S(1)} fusion(bf16[512,896]{1,0:T(8,128)(2,1)S(1)} %pad_maximum_fusion, s32[]{:T(128)S(6)} %select_n.38, bf16[128,512]{1,0:T(8,128)(2,1)} %copy-done.8, bf16[128,512]{1,0:T(8,128)(2,1)} %copy-done.7, bf16[128,512]{1,0:T(8,128)(2,1)S(1)} %slice.37, bf16[128,512]{1,0:T(8,128)(2,1)} %copy-done.9), kind=kOutput, calls=%fused_computation.18 | convolution fusion | flops 270532608 | bytes 2097156 | tf_op jit(solution)/shard_map/dot_general | solution.py:22
  77.1 0.6 collective-permute-done.3
  77.7 0.5 add_convert_fusion
  78.2 25.5 %all_to_all.15 = bf16[16,32,512]{2,1,0:T(8,128)(2,1)} all-to-all(bf16[16,32,512]{2,1,0:T(8,128)(2,1)S(1)} %bitcast.36), channel_id=1, replica_groups=mesh['y_hi'=2,'x'=4,'core'=2,'z'=16,'y_half'=2,'y_low'=2] {'y_hi','x','c..., dimensions={0} | all-to-all | bytes 1048576 | tf_op jit(solution)/shard_map/all_to_all | solution.py:136
  103.7 3.5 %shard_map.104 = (f32[1,32,3584]{2,1,0:T(8,128)}, bf16[1,32,3584]{2,1,0:T(8,128)(2,1)}, bf16[1,32,3584]{2,1,0:T(8,128)(2,1)}) custom-call(bf16[2,4,2,32,512]{4,3,2,1,0:T(8,128)(2,1)} %bitcast.37, f32[1,32,3584]{2,1,0:T(8,128)} %weight_ref.1, bf16[1,32,3584]{2,1,0:T(8,128)(2,1)} %moment_ref.1, bf16[1,32,3584]{2,1,0:T(8,128)(2,1)} %second_ref.1), custom_call_target="tpu_custom_call" | custom-call | tf_op jit(solution)/shard_map/pallas_call | solution.py:66
  (46 shorter events, 1.0 us)
Async XLA Ops:
  0.6 21.5 %copy-start = (s32[1,64,32]{1,2,0:T(8,128)S(1)}, s32[1,64,32]{1,2,0:T(8,128)}, u32[]{:S(2)}) copy-start(s32[1,64,32]{1,2,0:T(8,128)} %param.12) | copy-start | bytes 24580
  0.6 21.6 %copy-start.6 = (bf16[1,1,128,512]{3,2,1,0:T(8,128)(2,1)S(1)}, bf16[1,1,128,512]{3,2,1,0:T(8,128)(2,1)}, u32[]{:S(2)}) copy-start(bf16[1,1,128,512]{3,2,1,0:T(8,128)(2,1)} %param.8) | copy-start | bytes 393220
  0.7 22.2 %copy-start.4 = (bf16[1,1,128,3584]{3,2,1,0:T(8,128)(2,1)S(1)}, bf16[1,1,128,3584]{3,2,1,0:T(8,128)(2,1)}, u32[]{:S(2)}) copy-start(bf16[1,1,128,3584]{3,2,1,0:T(8,128)(2,1)} %param.11) | copy-start | bytes 2752516
  0.7 51.3 %all-to-all-start = ((bf16[32,2,3584]{2,1,0:T(2,128)(2,1)}), bf16[32,2,3584]{2,1,0:T(2,128)(2,1)S(1)}, u32[]{:S(2)}, u32[]{:S(2)}) async-start(bf16[32,2,3584]{2,1,0:T(2,128)(2,1)} %bitcast.38), calls=%async_computation | async-start | bytes 917504 | tf_op jit(solution)/shard_map/all_to_all | solution.py:94
  22.7 0.9 copy-start.5
  24.8 35.5 %collective-permute-start.2 = (bf16[128,1920]{1,0:T(8,128)(2,1)}, bf16[128,1920]{1,0:T(8,128)(2,1)S(1)}, u32[]{:S(2)}, u32[]{:S(2)}) collective-permute-start(bf16[128,1920]{1,0:T(8,128)(2,1)} %get-tuple-element.15), channel_id=1, source_target_pairs={{0,384},{128,0},{256,128},{384,256},{1,385},{129,1},{257,129},{385... | collective-permute-start | bytes 1474568 | tf_op jit(solution)/shard_map/ppermute | solution.py:110
  29.5 30.8 %collective-permute-start = (bf16[128,1920]{1,0:T(8,128)(2,1)}, bf16[128,1920]{1,0:T(8,128)(2,1)S(1)}, u32[]{:S(2)}, u32[]{:S(2)}) collective-permute-start(bf16[128,1920]{1,0:T(8,128)(2,1)} %get-tuple-element.16), channel_id=1, source_target_pairs={{0,128},{128,256},{256,384},{384,0},{1,129},{129,257},{257,385},{3... | collective-permute-start | bytes 1474568 | tf_op jit(solution)/shard_map/ppermute | solution.py:110
  31.4 28.9 %collective-permute-start.1 = (bf16[128,1920]{1,0:T(8,128)(2,1)S(1)}, bf16[128,1920]{1,0:T(8,128)(2,1)S(1)}, u32[]{:S(2)}, u32[]{:S(2)}) collective-permute-start(bf16[128,1920]{1,0:T(8,128)(2,1)S(1)} %get-tuple-element.17), channel_id=1, source_target_pairs={{0,256},{128,384},{256,0},{384,128},{1,257},{129,385},{257,1},{385... | collective-permute-start | bytes 1474568 | tf_op jit(solution)/shard_map/ppermute | solution.py:110
  55.0 17.5 %all-to-all-start.1 = ((bf16[8,64,896]{2,1,0:T(8,128)(2,1)}), bf16[8,64,896]{2,1,0:T(8,128)(2,1)S(1)}, u32[]{:S(2)}, u32[]{:S(2)}) async-start(bf16[8,64,896]{2,1,0:T(8,128)(2,1)} %shard_map.103), calls=%async_computation.1 | async-start | bytes 1835008 | tf_op jit(solution)/shard_map/all_to_all | solution.py:116
  60.3 0.9 copy-start.3
  60.3 1.1 %copy-start.1 = (bf16[128,1920]{1,0:T(8,128)(2,1)}, bf16[128,1920]{1,0:T(8,128)(2,1)S(1)}, u32[]{:S(2)}) copy-start(bf16[128,1920]{1,0:T(8,128)(2,1)S(1)} %collective-permute-done) | copy-start | bytes 1474564
  60.3 0.9 copy-start.2
  60.4 2.2 %copy-start.7 = (bf16[128,512]{1,0:T(8,128)(2,1)}, bf16[128,512]{1,0:T(8,128)(2,1)S(1)}, u32[]{:S(2)}) copy-start(bf16[128,512]{1,0:T(8,128)(2,1)S(1)} %slice.38) | copy-start | bytes 393220
  60.5 2.1 %copy-start.8 = (bf16[128,512]{1,0:T(8,128)(2,1)}, bf16[128,512]{1,0:T(8,128)(2,1)S(1)}, u32[]{:S(2)}) copy-start(bf16[128,512]{1,0:T(8,128)(2,1)S(1)} %slice.39) | copy-start | bytes 393220
  60.5 2.1 %copy-start.9 = (bf16[128,512]{1,0:T(8,128)(2,1)}, bf16[128,512]{1,0:T(8,128)(2,1)S(1)}, u32[]{:S(2)}) copy-start(bf16[128,512]{1,0:T(8,128)(2,1)S(1)} %slice.36) | copy-start | bytes 393220
  61.3 0.9 slice-start.2
  61.4 1.0 slice-start.1
  61.4 1.1 slice-start
  73.7 4.0 %collective-permute-start.3 = (bf16[512,512]{1,0:T(8,128)(2,1)}, bf16[512,512]{1,0:T(8,128)(2,1)S(1)}, u32[]{:S(2)}, u32[]{:S(2)}) collective-permute-start(bf16[512,512]{1,0:T(8,128)(2,1)} %fusion), channel_id=1, source_target_pairs={{0,64},{64,0},{1,65},{65,1},{2,66},{66,2},{3,67},{67,3},{4,68},{68... | collective-permute-start | bytes 1572872 | tf_op jit(solution)/shard_map/ppermute | solution.py:132

commit v4 on v3

--- a/solution.py
+++ b/solution.py
@@ -7,7 +7,8 @@
 
 AXES = ("y_hi", "x", "core", "z", "y_half", "y_low")
 N_X = 4
-TILE = 128
+OWNED = 32
+KERNEL_VMEM = 8 * 2**20
 
 beta_one = 0.9
 beta_two = 0.95
@@ -38,20 +39,17 @@
         out_shape=jax.ShapeDtypeStruct((2 * N_X, rows, span), near.dtype),
         in_specs=[pl.BlockSpec(memory_space=pltpu.VMEM)],
         out_specs=pl.BlockSpec(memory_space=pltpu.VMEM),
+        compiler_params=pltpu.CompilerParams(vmem_limit_bytes=KERNEL_VMEM),
     )(near)
 
 
 def adamw(sums, weight, moment, second):
-    rows, features = weight.shape[1:]
-    width = sums.shape[-1]
-    span = features // N_X
+    span = sums.shape[-1]
 
     def kernel(sums_ref, weight_ref, moment_ref, second_ref, new_weight, new_moment, new_second):
-        for j in range(2):
-            skip = j * (2 * width - span)
-            cols = slice(j * width, j * width + width - skip)
-            summed = sums_ref[0, 0, j, :, skip:].astype(jnp.float32)
-            summed = summed + sums_ref[1, 0, j, :, skip:].astype(jnp.float32)
+        for i in range(N_X):
+            cols = slice(i * span, (i + 1) * span)
+            summed = sums_ref[i].astype(jnp.float32) + sums_ref[N_X + i].astype(jnp.float32)
             first = beta_one * moment_ref[0, :, cols].astype(jnp.float32)
             first = first + (1.0 - beta_one) * summed
             next_ = beta_two * second_ref[0, :, cols].astype(jnp.float32)
@@ -62,18 +60,13 @@
             new_moment[0, :, cols] = first.astype(jnp.bfloat16)
             new_second[0, :, cols] = next_.astype(jnp.bfloat16)
 
-    shard = pl.BlockSpec((1, rows, span), lambda i: (0, 0, i))
+    vmem = pl.BlockSpec(memory_space=pltpu.VMEM)
     return pl.pallas_call(
         kernel,
-        grid=(N_X,),
         out_shape=tuple(jax.ShapeDtypeStruct(a.shape, a.dtype) for a in (weight, moment, second)),
-        in_specs=[
-            pl.BlockSpec((2, 1, 2, rows, width), lambda i: (0, i, 0, 0, 0)),
-            shard,
-            shard,
-            shard,
-        ],
-        out_specs=(shard, shard, shard),
+        in_specs=[vmem] * 4,
+        out_specs=(vmem,) * 3,
+        compiler_params=pltpu.CompilerParams(vmem_limit_bytes=KERNEL_VMEM),
     )(sums, weight, moment, second)
 
 
@@ -88,8 +81,7 @@
     hidden = hidden_acts[0, 0]
     rows, units = hidden.shape
     span = features // N_X
-    width = (span // TILE + 1) // 2 * TILE
-    shift = span - width
+    share = units // 2
 
     arrived = lax.all_to_all(outgoing, ("z", "y_half"), 0, 0, tiled=True)
 
@@ -116,25 +108,30 @@
     gathered = lax.all_to_all(blocks, ("x", "y_low"), 0, 0, tiled=True)
     gathered = gathered.reshape(-1, span)
 
+    def by_core(rows_of_units):
+        split = rows_of_units.reshape(-1, units // (2 * OWNED), 2, OWNED)
+        return split.transpose(0, 2, 1, 3).reshape(-1, units)
+
     back = jnp.stack([block[:, span : span + units] for block in held[::-1]])
     twice = jnp.concatenate([back, back])
     routed = lax.dynamic_slice_in_dim(twice, N_X - 1 - x, N_X, axis=0).reshape(-1, units)
-    owned = jnp.concatenate([block[:, span + units :] for block in held])
+    routed = by_core(routed)
+    owned = by_core(jnp.concatenate([block[:, span + units :] for block in held]))
     columns = jnp.concatenate([block[:, :span] for block in held])
 
     def partial_of(which):
-        start = which * shift
+        start = which * share
         return contract_rows(
-            owned, lax.dynamic_slice_in_dim(columns, start, width, axis=1)
-        ) + contract_rows(routed, lax.dynamic_slice_in_dim(gathered, start, width, axis=1))
+            lax.dynamic_slice_in_dim(owned, start, share, axis=1), columns
+        ) + contract_rows(lax.dynamic_slice_in_dim(routed, start, share, axis=1), gathered)
 
     other = partial_of(1 - core).astype(jnp.bfloat16)
     other = lax.ppermute(other, "core", [(0, 1), (1, 0)])
     partial = partial_of(core) + other.astype(jnp.float32)
 
-    partial = partial.astype(jnp.bfloat16).reshape(4 * N_X, -1, width)
-    partial = lax.all_to_all(partial, ("y_hi", "x", "core"), 0, 0, tiled=True)
-    return adamw(partial.reshape(2, N_X, 2, -1, width), weight, moment, second)
+    partial = partial.astype(jnp.bfloat16).reshape(2 * N_X, OWNED, span)
+    partial = lax.all_to_all(partial, ("y_hi", "x"), 0, 0, tiled=True)
+    return adamw(partial, weight, moment, second)
 
 
 def solution(mesh):

time: 108 us -> 101 us (0.935)
  waiting for transfers between devices: 26.4 us -> 22.8 us
  Pallas kernels: 5.57 us -> 2.35 us
  local copies, waits for them, and re-layouts: 4.11 us -> 6.34 us
  blocking collectives: 25.5 us -> 23.6 us
    all_to_all x1, waiting for transfers between devices: 9.36 us -> 6.65 us  [on_device(): gathered = lax.all_to_all(blocks, ('x', 'y_low'), 0, 0, tiled=True)]
    pallas_call x1, Pallas kernels: 3.55 us -> 1.35 us  [adamw(): pl.pallas_call(kernel, out_shape=tuple((jax.ShapeDtypeStruct(a.shape, a.d...]
    all_to_all x1, blocking collectives: 25.5 us -> 23.6 us  [on_device(): partial = lax.all_to_all(partial, ('y_hi', 'x'), 0, 0, tiled=True)]
    slice x7 -> x4, local copies, waits for them, and re-layouts: 1.01 us -> 2.83 us  [on_device(): columns = jnp.concatenate([block[:, :span] for block in held])]
  transfers between devices with their start and end apart: 6 -> 6, of which waited for: 3 -> 2; matrix products, arithmetic and copies ran while one was open for 5% -> 9% of each run, Pallas kernels for 2% -> 1%
where the time goes in v4:
time: 101 us; the launch traced here: 100 us
  starting transfers between devices  39.4 us (39%)
  blocking collectives  23.6 us (23%)
  waiting for transfers between devices  22.8 us (23%)
  local copies, waits for them, and re-layouts  6.34 us (6%)
  matrix products  3.09 us (3%)
  Pallas kernels  2.35 us (2%)
  other arithmetic  1.56 us (2%)
  between operations  1.1 us (1%)
    all_to_all x1, blocking collectives, on_device(): partial = lax.all_to_all(partial, ('y_hi', 'x'), 0, 0, tiled=True)  23.6 us
    all_to_all x1, starting transfers between devices, on_device(): arrived = lax.all_to_all(outgoing, ('z', 'y_half'), 0, 0, tiled=True)  21.4 us
    all_to_all x1, waiting for transfers between devices, on_device(): arrived = lax.all_to_all(outgoing, ('z', 'y_half'), 0, 0, tiled=True)  16.1 us
    ppermute x3, starting transfers between devices, on_device(): lax.ppermute(held[step], 'x', [(i, (i + step) % N_X) for i in range(N_X)])  10.8 us
    all_to_all x1, waiting for transfers between devices, on_device(): gathered = lax.all_to_all(blocks, ('x', 'y_low'), 0, 0, tiled=True)  6.65 us
    all_to_all x1, starting transfers between devices, on_device(): gathered = lax.all_to_all(blocks, ('x', 'y_low'), 0, 0, tiled=True)  5.31 us
    dot_general x4, matrix products, contract_rows(): lax.dot_general(left_rows, right_rows, (((0,), (0,)), ((), ())), preferre...  3.09 us
    slice x4, local copies, waits for them, and re-layouts, on_device(): columns = jnp.concatenate([block[:, :span] for block in held])  2.83 us
  transfers between devices with their start and end apart: 6, of which 2 were waited for; matrix products, arithmetic and copies ran while one was open for 9% of the time, Pallas kernels for 1%

profile of v4, /device:TPU:16, one launch (start us, length us, event | category | flops | bytes accessed | tf_op | source)
XLA Modules:
  0.0 100.3 jit_solution(10930447786274010215)
XLA Ops:
  0.7 21.4 %all-to-all-start = ((bf16[32,2,3584]{2,1,0:T(2,128)(2,1)}), bf16[32,2,3584]{2,1,0:T(2,128)(2,1)S(1)}, u32[]{:S(2)}, u32[]{:S(2)}) async-start(bf16[32,2,3584]{2,1,0:T(2,128)(2,1)} %bitcast.48), calls=%async_computation | async-start | bytes 917504 | tf_op jit(solution)/shard_map/all_to_all | solution.py:86
  22.5 0.2 fusion.9
  23.9 1.2 %pad_maximum_fusion.1 = (bf16[128,1920]{0,1:T(8,128)(2,1)}, bf16[128,1920]{0,1:T(8,128)(2,1)}, bf16[128,1920]{0,1:T(8,128)(2,1)S(1)}, bf16[128,1920]{0,1:T(8,128)(2,1)S(1)}) fusion(bf16[128,512]{0,1:T(8,128)(2,1)S(1)} %bitcast.45, bf16[128,512]{0,1:T(8,128)(2,1)S(1)} %copy.26, bf16[128,896]{0,1:T(8,128)(2,1)S(1)} %bitcast.41, ...), kind=kLoop, calls=%fused_computation.5 | loop fusion | flops 4423680 | bytes 3145728 | tf_op jit(solution)/shard_map/concatenate | solution.py:100
  25.1 4.7 %collective-permute-start.2 = (bf16[128,1920]{0,1:T(8,128)(2,1)}, bf16[128,1920]{0,1:T(8,128)(2,1)S(1)}, u32[]{:S(2)}, u32[]{:S(2)}) collective-permute-start(bf16[128,1920]{0,1:T(8,128)(2,1)} %get-tuple-element.15), channel_id=1, source_target_pairs={{0,384},{128,0},{256,128},{384,256},{1,385},{129,1},{257,129},{385... | collective-permute-start | bytes 1474568 | tf_op jit(solution)/shard_map/ppermute | solution.py:102
  29.8 1.9 %collective-permute-start = (bf16[128,1920]{0,1:T(8,128)(2,1)}, bf16[128,1920]{0,1:T(8,128)(2,1)S(1)}, u32[]{:S(2)}, u32[]{:S(2)}) collective-permute-start(bf16[128,1920]{0,1:T(8,128)(2,1)} %get-tuple-element.16), channel_id=1, source_target_pairs={{0,128},{128,256},{256,384},{384,0},{1,129},{129,257},{257,385},{3... | collective-permute-start | bytes 1474568 | tf_op jit(solution)/shard_map/ppermute | solution.py:102
  31.7 4.2 %collective-permute-start.1 = (bf16[128,1920]{0,1:T(8,128)(2,1)S(1)}, bf16[128,1920]{0,1:T(8,128)(2,1)S(1)}, u32[]{:S(2)}, u32[]{:S(2)}) collective-permute-start(bf16[128,1920]{0,1:T(8,128)(2,1)S(1)} %get-tuple-element.17), channel_id=1, source_target_pairs={{0,256},{128,384},{256,0},{384,128},{1,257},{129,385},{257,1},{385... | collective-permute-start | bytes 1474568 | tf_op jit(solution)/shard_map/ppermute | solution.py:102
  35.9 16.1 %all-to-all-done = bf16[32,2,3584]{2,1,0:T(2,128)(2,1)S(1)} async-done(((bf16[32,2,3584]{2,1,0:T(2,128)(2,1)}), bf16[32,2,3584]{2,1,0:T(2,128)(2,1)S(1)}, u32[]{:S(2)}, u32[]{:S(2)}) %all-to-all-start) | async-done | bytes 458784 | tf_op jit(solution)/shard_map/all_to_all | solution.py:86
  52.2 1.0 %shard_map.103 = bf16[8,64,896]{2,1,0:T(8,128)(2,1)} custom-call(bf16[64,3584]{1,0:T(8,128)(2,1)S(1)} %reshape.59.near_ref), custom_call_target="tpu_custom_call" | custom-call | tf_op jit(solution)/shard_map/pallas_call | solution.py:37
  53.2 5.3 %all-to-all-start.1 = ((bf16[8,64,896]{2,1,0:T(8,128)(2,1)}), bf16[8,64,896]{2,1,0:T(8,128)(2,1)S(1)}, u32[]{:S(2)}, u32[]{:S(2)}) async-start(bf16[8,64,896]{2,1,0:T(8,128)(2,1)} %shard_map.103), calls=%async_computation.1 | async-start | bytes 1835008 | tf_op jit(solution)/shard_map/all_to_all | solution.py:108
  58.5 0.7 slice.40
  59.3 0.7 slice.41
  60.0 0.7 slice.42
  60.7 0.7 slice.43
  61.8 0.4 copy.34
  62.2 0.2 reshape_reshape.3
  62.5 0.6 copy-done.5
  63.5 0.5 fusion.2
  64.0 6.6 %all-to-all-done.1 = bf16[8,64,896]{2,1,0:T(8,128)(2,1)S(1)} async-done(((bf16[8,64,896]{2,1,0:T(8,128)(2,1)}), bf16[8,64,896]{2,1,0:T(8,128)(2,1)S(1)}, u32[]{:S(2)}, u32[]{:S(2)}) %all-to-all-start.1) | async-done | bytes 917536 | tf_op jit(solution)/shard_map/all_to_all | solution.py:108
  70.7 0.4 fusion
  71.1 1.9 %collective-permute-start.3 = (bf16[256,896]{1,0:T(8,128)(2,1)S(1)}, bf16[256,896]{1,0:T(8,128)(2,1)S(1)}, u32[]{:S(2)}, u32[]{:S(2)}) collective-permute-start(bf16[256,896]{1,0:T(8,128)(2,1)S(1)} %fusion), channel_id=1, source_target_pairs={{0,64},{64,0},{1,65},{65,1},{2,66},{66,2},{3,67},{67,3},{4,68},{68... | collective-permute-start | bytes 1376264 | tf_op jit(solution)/shard_map/ppermute | solution.py:129
  73.0 1.7 %fusion.7 = f32[256,896]{1,0:T(8,128)S(1)} fusion(bf16[512,512]{0,1:T(8,128)(2,1)S(1)} %bitcast.47, s32[]{:T(128)S(6)} %select_n.38, bf16[128,896]{0,1:T(8,128)(2,1)} %slice.43, bf16[128,896]{0,1:T(8,128)(2,1)} %slice.42, bf16[128,896]{0,1:T(8,128)(2,1)} %slice.41, bf16[128,896]{0,1:T(8,128)(2,1)} %slice.40), kind=kOutput, calls=%fused_computation.18 | convolution fusion | flops 238551040 | bytes 2097156 | tf_op jit(solution)/shard_map/dot_general | solution.py:23
  74.8 0.4 add_convert_fusion
  75.3 23.6 %all_to_all.15.sums_ref = bf16[8,32,896]{2,1,0:T(8,128)(2,1)S(1)} all-to-all(bf16[8,32,896]{2,1,0:T(8,128)(2,1)S(1)} %bitcast.40), channel_id=1, replica_groups=mesh['y_hi'=2,'x'=4,'core'=2,'z'=16,'y_half'=2,'y_low'=2] {'y_hi','x'}, dimensions={0} | all-to-all | bytes 917504 | tf_op jit(solution)/shard_map/all_to_all | solution.py:133
  98.9 1.3 %shard_map.104 = (f32[1,32,3584]{2,1,0:T(8,128)}, bf16[1,32,3584]{2,1,0:T(8,128)(2,1)}, bf16[1,32,3584]{2,1,0:T(8,128)(2,1)}) custom-call(bf16[8,32,896]{2,1,0:T(8,128)(2,1)S(1)} %all_to_all.15.sums_ref, f32[1,32,3584]{2,1,0:T(8,128)S(1)} %copy-done.1, bf16[1,32,3584]{2,1,0:T(8,128)(2,1)S(1)} %copy-done.2, bf16[1,32,3584]{2,1,0:T(8,128)(2,1)S(1)} %copy-done.3), custom_call_target="tpu_custom_call" | custom-call | tf_op jit(solution)/shard_map/pallas_call | solution.py:64
  (55 shorter events, 2.4 us)
Async XLA Ops:
  0.6 21.5 %copy-start = (s32[1,64,32]{1,2,0:T(8,128)S(1)}, s32[1,64,32]{1,2,0:T(8,128)}, u32[]{:S(2)}) copy-start(s32[1,64,32]{1,2,0:T(8,128)} %param.12) | copy-start | bytes 24580
  0.6 21.7 %copy-start.9 = (bf16[1,1,128,512]{3,2,1,0:T(8,128)(2,1)S(1)}, bf16[1,1,128,512]{3,2,1,0:T(8,128)(2,1)}, u32[]{:S(2)}) copy-start(bf16[1,1,128,512]{3,2,1,0:T(8,128)(2,1)} %param.8) | copy-start | bytes 393220
  0.7 22.2 %copy-start.10 = (bf16[1,1,128,512]{3,2,1,0:T(8,128)(2,1)S(1)}, bf16[1,1,128,512]{3,2,1,0:T(8,128)(2,1)}, u32[]{:S(2)}) copy-start(bf16[1,1,128,512]{3,2,1,0:T(8,128)(2,1)} %param.10) | copy-start | bytes 393220
  0.7 22.4 %copy-start.4 = (bf16[1,1,128,3584]{3,2,1,0:T(8,128)(2,1)S(1)}, bf16[1,1,128,3584]{3,2,1,0:T(8,128)(2,1)}, u32[]{:S(2)}) copy-start(bf16[1,1,128,3584]{3,2,1,0:T(8,128)(2,1)} %param.11) | copy-start | bytes 2752516
  0.7 51.3 %all-to-all-start = ((bf16[32,2,3584]{2,1,0:T(2,128)(2,1)}), bf16[32,2,3584]{2,1,0:T(2,128)(2,1)S(1)}, u32[]{:S(2)}, u32[]{:S(2)}) async-start(bf16[32,2,3584]{2,1,0:T(2,128)(2,1)} %bitcast.48), calls=%async_computation | async-start | bytes 917504 | tf_op jit(solution)/shard_map/all_to_all | solution.py:86
  25.1 33.4 %collective-permute-start.2 = (bf16[128,1920]{0,1:T(8,128)(2,1)}, bf16[128,1920]{0,1:T(8,128)(2,1)S(1)}, u32[]{:S(2)}, u32[]{:S(2)}) collective-permute-start(bf16[128,1920]{0,1:T(8,128)(2,1)} %get-tuple-element.15), channel_id=1, source_target_pairs={{0,384},{128,0},{256,128},{384,256},{1,385},{129,1},{257,129},{385... | collective-permute-start | bytes 1474568 | tf_op jit(solution)/shard_map/ppermute | solution.py:102
  29.8 28.8 %collective-permute-start = (bf16[128,1920]{0,1:T(8,128)(2,1)}, bf16[128,1920]{0,1:T(8,128)(2,1)S(1)}, u32[]{:S(2)}, u32[]{:S(2)}) collective-permute-start(bf16[128,1920]{0,1:T(8,128)(2,1)} %get-tuple-element.16), channel_id=1, source_target_pairs={{0,128},{128,256},{256,384},{384,0},{1,129},{129,257},{257,385},{3... | collective-permute-start | bytes 1474568 | tf_op jit(solution)/shard_map/ppermute | solution.py:102
  31.7 26.8 %collective-permute-start.1 = (bf16[128,1920]{0,1:T(8,128)(2,1)S(1)}, bf16[128,1920]{0,1:T(8,128)(2,1)S(1)}, u32[]{:S(2)}, u32[]{:S(2)}) collective-permute-start(bf16[128,1920]{0,1:T(8,128)(2,1)S(1)} %get-tuple-element.17), channel_id=1, source_target_pairs={{0,256},{128,384},{256,0},{384,128},{1,257},{129,385},{257,1},{385... | collective-permute-start | bytes 1474568 | tf_op jit(solution)/shard_map/ppermute | solution.py:102
  53.2 17.5 %all-to-all-start.1 = ((bf16[8,64,896]{2,1,0:T(8,128)(2,1)}), bf16[8,64,896]{2,1,0:T(8,128)(2,1)S(1)}, u32[]{:S(2)}, u32[]{:S(2)}) async-start(bf16[8,64,896]{2,1,0:T(8,128)(2,1)} %shard_map.103), calls=%async_computation.1 | async-start | bytes 1835008 | tf_op jit(solution)/shard_map/all_to_all | solution.py:108
  62.2 0.9 copy-start.5
  62.2 1.0 %copy-start.6 = (bf16[128,896]{0,1:T(8,128)(2,1)S(1)}, bf16[128,896]{0,1:T(8,128)(2,1)}, u32[]{:S(2)}) copy-start(bf16[128,896]{0,1:T(8,128)(2,1)} %slice.41) | copy-start | bytes 688132
  62.4 1.0 copy-start.7
  62.4 1.1 %copy-start.8 = (bf16[128,896]{0,1:T(8,128)(2,1)S(1)}, bf16[128,896]{0,1:T(8,128)(2,1)}, u32[]{:S(2)}) copy-start(bf16[128,896]{0,1:T(8,128)(2,1)} %slice.43) | copy-start | bytes 688132
  71.1 3.7 %collective-permute-start.3 = (bf16[256,896]{1,0:T(8,128)(2,1)S(1)}, bf16[256,896]{1,0:T(8,128)(2,1)S(1)}, u32[]{:S(2)}, u32[]{:S(2)}) collective-permute-start(bf16[256,896]{1,0:T(8,128)(2,1)S(1)} %fusion), channel_id=1, source_target_pairs={{0,64},{64,0},{1,65},{65,1},{2,66},{66,2},{3,67},{67,3},{4,68},{68... | collective-permute-start | bytes 1376264 | tf_op jit(solution)/shard_map/ppermute | solution.py:129
  75.3 23.7 %copy-start.1 = (f32[1,32,3584]{2,1,0:T(8,128)S(1)}, f32[1,32,3584]{2,1,0:T(8,128)}, u32[]{:S(2)}) copy-start(f32[1,32,3584]{2,1,0:T(8,128)} %weight_ref.1) | copy-start | bytes 1376260
  75.3 23.7 %copy-start.2 = (bf16[1,32,3584]{2,1,0:T(8,128)(2,1)S(1)}, bf16[1,32,3584]{2,1,0:T(8,128)(2,1)}, u32[]{:S(2)}) copy-start(bf16[1,32,3584]{2,1,0:T(8,128)(2,1)} %moment_ref.1) | copy-start | bytes 688132
  75.3 23.6 %copy-start.3 = (bf16[1,32,3584]{2,1,0:T(8,128)(2,1)S(1)}, bf16[1,32,3584]{2,1,0:T(8,128)(2,1)}, u32[]{:S(2)}) copy-start(bf16[1,32,3584]{2,1,0:T(8,128)(2,1)} %second_ref.1) | copy-start | bytes 688132

commit v5 on v4

--- a/solution.py
+++ b/solution.py
@@ -28,17 +28,25 @@
 def column_blocks(near, span):
     rows = near.shape[0]
 
-    def kernel(near_ref, out_ref):
-        for i in range(N_X):
-            block = near_ref[:, i * span : (i + 1) * span]
-            for j in range(2):
-                out_ref[2 * i + j] = block
+    def kernel(near_ref, out_ref, sems):
+        copies = [
+            pltpu.make_async_copy(
+                near_ref.at[:, i * span : (i + 1) * span], out_ref.at[2 * i + j], sems.at[i, j]
+            )
+            for i in range(N_X)
+            for j in range(2)
+        ]
+        for copy in copies:
+            copy.start()
+        for copy in copies:
+            copy.wait()
 
     return pl.pallas_call(
         kernel,
         out_shape=jax.ShapeDtypeStruct((2 * N_X, rows, span), near.dtype),
         in_specs=[pl.BlockSpec(memory_space=pltpu.VMEM)],
-        out_specs=pl.BlockSpec(memory_space=pltpu.VMEM),
+        out_specs=pl.BlockSpec(memory_space=pl.ANY),
+        scratch_shapes=[pltpu.SemaphoreType.DMA((N_X, 2))],
         compiler_params=pltpu.CompilerParams(vmem_limit_bytes=KERNEL_VMEM),
     )(near)
 
@@ -46,7 +54,11 @@
 def adamw(sums, weight, moment, second):
     span = sums.shape[-1]
 
-    def kernel(sums_ref, weight_ref, moment_ref, second_ref, new_weight, new_moment, new_second):
+    rows = weight.shape[1]
+
+    def kernel(sums_ref, weight_ref, moment_ref, second_ref, *rest):
+        outs, held, sems = rest[:3], rest[3:6], rest[6]
+        copies = []
         for i in range(N_X):
             cols = slice(i * span, (i + 1) * span)
             summed = sums_ref[i].astype(jnp.float32) + sums_ref[N_X + i].astype(jnp.float32)
@@ -54,20 +66,30 @@
             first = first + (1.0 - beta_one) * summed
             next_ = beta_two * second_ref[0, :, cols].astype(jnp.float32)
             next_ = next_ + (1.0 - beta_two) * summed * summed
-            direction = first / correct_one / (jnp.sqrt(next_ / correct_two) + epsilon)
+            root = jnp.sqrt(next_ * (1.0 / correct_two)) + epsilon
+            direction = first * (1.0 / correct_one) / root
             master = weight_ref[0, :, cols]
-            new_weight[0, :, cols] = master - learn_rate * (direction + decay_rate * master)
-            new_moment[0, :, cols] = first.astype(jnp.bfloat16)
-            new_second[0, :, cols] = next_.astype(jnp.bfloat16)
+            held[0][i] = master - learn_rate * (direction + decay_rate * master)
+            held[1][i] = first.astype(jnp.bfloat16)
+            held[2][i] = next_.astype(jnp.bfloat16)
+            for j in range(3):
+                copies.append(
+                    pltpu.make_async_copy(held[j].at[i], outs[j].at[0, :, cols], sems.at[j, i])
+                )
+                copies[-1].start()
+        for copy in copies:
+            copy.wait()
 
-    vmem = pl.BlockSpec(memory_space=pltpu.VMEM)
+    arrays = (weight, moment, second)
     return pl.pallas_call(
         kernel,
-        out_shape=tuple(jax.ShapeDtypeStruct(a.shape, a.dtype) for a in (weight, moment, second)),
-        in_specs=[vmem] * 4,
-        out_specs=(vmem,) * 3,
+        out_shape=tuple(jax.ShapeDtypeStruct(a.shape, a.dtype) for a in arrays),
+        in_specs=[pl.BlockSpec(memory_space=pltpu.VMEM)] * 4,
+        out_specs=(pl.BlockSpec(memory_space=pl.ANY),) * 3,
+        scratch_shapes=[pltpu.VMEM((N_X, rows, span), a.dtype) for a in arrays]
+        + [pltpu.SemaphoreType.DMA((3, N_X))],
         compiler_params=pltpu.CompilerParams(vmem_limit_bytes=KERNEL_VMEM),
-    )(sums, weight, moment, second)
+    )(sums, *arrays)
 
 
 def on_device(

time: 101 us -> 101 us (level)
  no operation moved by 1% of the time
where the time goes in v5:
time: 101 us; the launch traced here: 100 us
  starting transfers between devices  39.4 us (39%)
  blocking collectives  23.6 us (23%)
  waiting for transfers between devices  22.8 us (23%)
  local copies, waits for them, and re-layouts  6.34 us (6%)
  matrix products  3.09 us (3%)
  Pallas kernels  2.25 us (2%)
  other arithmetic  1.56 us (2%)
  between operations  1.11 us (1%)
    all_to_all x1, blocking collectives, on_device(): partial = lax.all_to_all(partial, ('y_hi', 'x'), 0, 0, tiled=True)  23.6 us
    all_to_all x1, starting transfers between devices, on_device(): arrived = lax.all_to_all(outgoing, ('z', 'y_half'), 0, 0, tiled=True)  21.4 us
    all_to_all x1, waiting for transfers between devices, on_device(): arrived = lax.all_to_all(outgoing, ('z', 'y_half'), 0, 0, tiled=True)  16.1 us
    ppermute x3, starting transfers between devices, on_device(): lax.ppermute(held[step], 'x', [(i, (i + step) % N_X) for i in range(N_X)])  10.8 us
    all_to_all x1, waiting for transfers between devices, on_device(): gathered = lax.all_to_all(blocks, ('x', 'y_low'), 0, 0, tiled=True)  6.65 us
    all_to_all x1, starting transfers between devices, on_device(): gathered = lax.all_to_all(blocks, ('x', 'y_low'), 0, 0, tiled=True)  5.32 us
    dot_general x4, matrix products, contract_rows(): lax.dot_general(left_rows, right_rows, (((0,), (0,)), ((), ())), preferre...  3.09 us
    slice x4, local copies, waits for them, and re-layouts, on_device(): columns = jnp.concatenate([block[:, :span] for block in held])  2.83 us
  transfers between devices with their start and end apart: 6, of which 2 were waited for; matrix products, arithmetic and copies ran while one was open for 9% of the time, Pallas kernels for 1%

profile of v5, /device:TPU:16, one launch (start us, length us, event | category | flops | bytes accessed | tf_op | source)
XLA Modules:
  0.0 100.2 jit_solution(15629905155964020533)
XLA Ops:
  0.7 21.4 %all-to-all-start = ((bf16[32,2,3584]{2,1,0:T(2,128)(2,1)}), bf16[32,2,3584]{2,1,0:T(2,128)(2,1)S(1)}, u32[]{:S(2)}, u32[]{:S(2)}) async-start(bf16[32,2,3584]{2,1,0:T(2,128)(2,1)} %bitcast.48), calls=%async_computation | async-start | bytes 917504 | tf_op jit(solution)/shard_map/all_to_all | solution.py:108
  22.5 0.2 fusion.9
  23.9 1.2 %pad_maximum_fusion.1 = (bf16[128,1920]{0,1:T(8,128)(2,1)}, bf16[128,1920]{0,1:T(8,128)(2,1)}, bf16[128,1920]{0,1:T(8,128)(2,1)S(1)}, bf16[128,1920]{0,1:T(8,128)(2,1)S(1)}) fusion(bf16[128,512]{0,1:T(8,128)(2,1)S(1)} %bitcast.45, bf16[128,512]{0,1:T(8,128)(2,1)S(1)} %copy.26, bf16[128,896]{0,1:T(8,128)(2,1)S(1)} %bitcast.41, ...), kind=kLoop, calls=%fused_computation.5 | loop fusion | flops 4423680 | bytes 3145728 | tf_op jit(solution)/shard_map/concatenate | solution.py:122
  25.1 4.7 %collective-permute-start.2 = (bf16[128,1920]{0,1:T(8,128)(2,1)}, bf16[128,1920]{0,1:T(8,128)(2,1)S(1)}, u32[]{:S(2)}, u32[]{:S(2)}) collective-permute-start(bf16[128,1920]{0,1:T(8,128)(2,1)} %get-tuple-element.15), channel_id=1, source_target_pairs={{0,384},{128,0},{256,128},{384,256},{1,385},{129,1},{257,129},{385... | collective-permute-start | bytes 1474568 | tf_op jit(solution)/shard_map/ppermute | solution.py:124
  29.8 1.9 %collective-permute-start = (bf16[128,1920]{0,1:T(8,128)(2,1)}, bf16[128,1920]{0,1:T(8,128)(2,1)S(1)}, u32[]{:S(2)}, u32[]{:S(2)}) collective-permute-start(bf16[128,1920]{0,1:T(8,128)(2,1)} %get-tuple-element.16), channel_id=1, source_target_pairs={{0,128},{128,256},{256,384},{384,0},{1,129},{129,257},{257,385},{3... | collective-permute-start | bytes 1474568 | tf_op jit(solution)/shard_map/ppermute | solution.py:124
  31.7 4.2 %collective-permute-start.1 = (bf16[128,1920]{0,1:T(8,128)(2,1)S(1)}, bf16[128,1920]{0,1:T(8,128)(2,1)S(1)}, u32[]{:S(2)}, u32[]{:S(2)}) collective-permute-start(bf16[128,1920]{0,1:T(8,128)(2,1)S(1)} %get-tuple-element.17), channel_id=1, source_target_pairs={{0,256},{128,384},{256,0},{384,128},{1,257},{129,385},{257,1},{385... | collective-permute-start | bytes 1474568 | tf_op jit(solution)/shard_map/ppermute | solution.py:124
  35.9 16.1 %all-to-all-done = bf16[32,2,3584]{2,1,0:T(2,128)(2,1)S(1)} async-done(((bf16[32,2,3584]{2,1,0:T(2,128)(2,1)}), bf16[32,2,3584]{2,1,0:T(2,128)(2,1)S(1)}, u32[]{:S(2)}, u32[]{:S(2)}) %all-to-all-start) | async-done | bytes 458784 | tf_op jit(solution)/shard_map/all_to_all | solution.py:108
  52.2 1.0 %shard_map.103 = bf16[8,64,896]{2,1,0:T(8,128)(2,1)} custom-call(bf16[64,3584]{1,0:T(8,128)(2,1)S(1)} %reshape.59.near_ref), custom_call_target="tpu_custom_call" | custom-call | tf_op jit(solution)/shard_map/pallas_call | solution.py:44
  53.2 5.3 %all-to-all-start.1 = ((bf16[8,64,896]{2,1,0:T(8,128)(2,1)}), bf16[8,64,896]{2,1,0:T(8,128)(2,1)S(1)}, u32[]{:S(2)}, u32[]{:S(2)}) async-start(bf16[8,64,896]{2,1,0:T(8,128)(2,1)} %shard_map.103), calls=%async_computation.1 | async-start | bytes 1835008 | tf_op jit(solution)/shard_map/all_to_all | solution.py:130
  58.6 0.7 slice.40
  59.3 0.7 slice.41
  60.0 0.7 slice.42
  60.7 0.7 slice.43
  61.8 0.4 copy.34
  62.3 0.2 reshape_reshape.3
  62.5 0.6 copy-done.5
  63.6 0.5 fusion.2
  64.0 6.6 %all-to-all-done.1 = bf16[8,64,896]{2,1,0:T(8,128)(2,1)S(1)} async-done(((bf16[8,64,896]{2,1,0:T(8,128)(2,1)}), bf16[8,64,896]{2,1,0:T(8,128)(2,1)S(1)}, u32[]{:S(2)}, u32[]{:S(2)}) %all-to-all-start.1) | async-done | bytes 917536 | tf_op jit(solution)/shard_map/all_to_all | solution.py:130
  70.7 0.4 fusion
  71.1 1.9 %collective-permute-start.3 = (bf16[256,896]{1,0:T(8,128)(2,1)S(1)}, bf16[256,896]{1,0:T(8,128)(2,1)S(1)}, u32[]{:S(2)}, u32[]{:S(2)}) collective-permute-start(bf16[256,896]{1,0:T(8,128)(2,1)S(1)} %fusion), channel_id=1, source_target_pairs={{0,64},{64,0},{1,65},{65,1},{2,66},{66,2},{3,67},{67,3},{4,68},{68... | collective-permute-start | bytes 1376264 | tf_op jit(solution)/shard_map/ppermute | solution.py:151
  73.0 1.7 %fusion.7 = f32[256,896]{1,0:T(8,128)S(1)} fusion(bf16[512,512]{0,1:T(8,128)(2,1)S(1)} %bitcast.47, s32[]{:T(128)S(6)} %select_n.38, bf16[128,896]{0,1:T(8,128)(2,1)} %slice.43, bf16[128,896]{0,1:T(8,128)(2,1)} %slice.42, bf16[128,896]{0,1:T(8,128)(2,1)} %slice.41, bf16[128,896]{0,1:T(8,128)(2,1)} %slice.40), kind=kOutput, calls=%fused_computation.18 | convolution fusion | flops 238551040 | bytes 2097156 | tf_op jit(solution)/shard_map/dot_general | solution.py:23
  74.8 0.4 add_convert_fusion
  75.3 23.6 %all_to_all.15.sums_ref = bf16[8,32,896]{2,1,0:T(8,128)(2,1)S(1)} all-to-all(bf16[8,32,896]{2,1,0:T(8,128)(2,1)S(1)} %bitcast.40), channel_id=1, replica_groups=mesh['y_hi'=2,'x'=4,'core'=2,'z'=16,'y_half'=2,'y_low'=2] {'y_hi','x'}, dimensions={0} | all-to-all | bytes 917504 | tf_op jit(solution)/shard_map/all_to_all | solution.py:155
  99.0 1.2 %shard_map.104 = (f32[1,32,3584]{2,1,0:T(8,128)}, bf16[1,32,3584]{2,1,0:T(8,128)(2,1)}, bf16[1,32,3584]{2,1,0:T(8,128)(2,1)}) custom-call(bf16[8,32,896]{2,1,0:T(8,128)(2,1)S(1)} %all_to_all.15.sums_ref, f32[1,32,3584]{2,1,0:T(8,128)S(1)} %copy-done.1, bf16[1,32,3584]{2,1,0:T(8,128)(2,1)S(1)} %copy-done.2, bf16[1,32,3584]{2,1,0:T(8,128)(2,1)S(1)} %copy-done.3), custom_call_target="tpu_custom_call" | custom-call | tf_op jit(solution)/shard_map/pallas_call | solution.py:84
  (55 shorter events, 2.4 us)
Async XLA Ops:
  0.6 21.5 %copy-start = (s32[1,64,32]{1,2,0:T(8,128)S(1)}, s32[1,64,32]{1,2,0:T(8,128)}, u32[]{:S(2)}) copy-start(s32[1,64,32]{1,2,0:T(8,128)} %param.12) | copy-start | bytes 24580
  0.6 21.7 %copy-start.9 = (bf16[1,1,128,512]{3,2,1,0:T(8,128)(2,1)S(1)}, bf16[1,1,128,512]{3,2,1,0:T(8,128)(2,1)}, u32[]{:S(2)}) copy-start(bf16[1,1,128,512]{3,2,1,0:T(8,128)(2,1)} %param.8) | copy-start | bytes 393220
  0.7 22.2 %copy-start.10 = (bf16[1,1,128,512]{3,2,1,0:T(8,128)(2,1)S(1)}, bf16[1,1,128,512]{3,2,1,0:T(8,128)(2,1)}, u32[]{:S(2)}) copy-start(bf16[1,1,128,512]{3,2,1,0:T(8,128)(2,1)} %param.10) | copy-start | bytes 393220
  0.7 22.4 %copy-start.4 = (bf16[1,1,128,3584]{3,2,1,0:T(8,128)(2,1)S(1)}, bf16[1,1,128,3584]{3,2,1,0:T(8,128)(2,1)}, u32[]{:S(2)}) copy-start(bf16[1,1,128,3584]{3,2,1,0:T(8,128)(2,1)} %param.11) | copy-start | bytes 2752516
  0.7 51.3 %all-to-all-start = ((bf16[32,2,3584]{2,1,0:T(2,128)(2,1)}), bf16[32,2,3584]{2,1,0:T(2,128)(2,1)S(1)}, u32[]{:S(2)}, u32[]{:S(2)}) async-start(bf16[32,2,3584]{2,1,0:T(2,128)(2,1)} %bitcast.48), calls=%async_computation | async-start | bytes 917504 | tf_op jit(solution)/shard_map/all_to_all | solution.py:108
  25.1 33.4 %collective-permute-start.2 = (bf16[128,1920]{0,1:T(8,128)(2,1)}, bf16[128,1920]{0,1:T(8,128)(2,1)S(1)}, u32[]{:S(2)}, u32[]{:S(2)}) collective-permute-start(bf16[128,1920]{0,1:T(8,128)(2,1)} %get-tuple-element.15), channel_id=1, source_target_pairs={{0,384},{128,0},{256,128},{384,256},{1,385},{129,1},{257,129},{385... | collective-permute-start | bytes 1474568 | tf_op jit(solution)/shard_map/ppermute | solution.py:124
  29.8 28.8 %collective-permute-start = (bf16[128,1920]{0,1:T(8,128)(2,1)}, bf16[128,1920]{0,1:T(8,128)(2,1)S(1)}, u32[]{:S(2)}, u32[]{:S(2)}) collective-permute-start(bf16[128,1920]{0,1:T(8,128)(2,1)} %get-tuple-element.16), channel_id=1, source_target_pairs={{0,128},{128,256},{256,384},{384,0},{1,129},{129,257},{257,385},{3... | collective-permute-start | bytes 1474568 | tf_op jit(solution)/shard_map/ppermute | solution.py:124
  31.7 26.9 %collective-permute-start.1 = (bf16[128,1920]{0,1:T(8,128)(2,1)S(1)}, bf16[128,1920]{0,1:T(8,128)(2,1)S(1)}, u32[]{:S(2)}, u32[]{:S(2)}) collective-permute-start(bf16[128,1920]{0,1:T(8,128)(2,1)S(1)} %get-tuple-element.17), channel_id=1, source_target_pairs={{0,256},{128,384},{256,0},{384,128},{1,257},{129,385},{257,1},{385... | collective-permute-start | bytes 1474568 | tf_op jit(solution)/shard_map/ppermute | solution.py:124
  53.2 17.5 %all-to-all-start.1 = ((bf16[8,64,896]{2,1,0:T(8,128)(2,1)}), bf16[8,64,896]{2,1,0:T(8,128)(2,1)S(1)}, u32[]{:S(2)}, u32[]{:S(2)}) async-start(bf16[8,64,896]{2,1,0:T(8,128)(2,1)} %shard_map.103), calls=%async_computation.1 | async-start | bytes 1835008 | tf_op jit(solution)/shard_map/all_to_all | solution.py:130
  62.2 0.9 copy-start.5
  62.2 1.0 %copy-start.6 = (bf16[128,896]{0,1:T(8,128)(2,1)S(1)}, bf16[128,896]{0,1:T(8,128)(2,1)}, u32[]{:S(2)}) copy-start(bf16[128,896]{0,1:T(8,128)(2,1)} %slice.41) | copy-start | bytes 688132
  62.5 1.0 copy-start.7
  62.5 1.1 %copy-start.8 = (bf16[128,896]{0,1:T(8,128)(2,1)S(1)}, bf16[128,896]{0,1:T(8,128)(2,1)}, u32[]{:S(2)}) copy-start(bf16[128,896]{0,1:T(8,128)(2,1)} %slice.43) | copy-start | bytes 688132
  71.1 3.7 %collective-permute-start.3 = (bf16[256,896]{1,0:T(8,128)(2,1)S(1)}, bf16[256,896]{1,0:T(8,128)(2,1)S(1)}, u32[]{:S(2)}, u32[]{:S(2)}) collective-permute-start(bf16[256,896]{1,0:T(8,128)(2,1)S(1)} %fusion), channel_id=1, source_target_pairs={{0,64},{64,0},{1,65},{65,1},{2,66},{66,2},{3,67},{67,3},{4,68},{68... | collective-permute-start | bytes 1376264 | tf_op jit(solution)/shard_map/ppermute | solution.py:151
  75.3 23.7 %copy-start.1 = (f32[1,32,3584]{2,1,0:T(8,128)S(1)}, f32[1,32,3584]{2,1,0:T(8,128)}, u32[]{:S(2)}) copy-start(f32[1,32,3584]{2,1,0:T(8,128)} %weight_ref.1) | copy-start | bytes 1376260
  75.3 23.7 %copy-start.2 = (bf16[1,32,3584]{2,1,0:T(8,128)(2,1)S(1)}, bf16[1,32,3584]{2,1,0:T(8,128)(2,1)}, u32[]{:S(2)}) copy-start(bf16[1,32,3584]{2,1,0:T(8,128)(2,1)} %moment_ref.1) | copy-start | bytes 688132
  75.3 23.7 %copy-start.3 = (bf16[1,32,3584]{2,1,0:T(8,128)(2,1)S(1)}, bf16[1,32,3584]{2,1,0:T(8,128)(2,1)}, u32[]{:S(2)}) copy-start(bf16[1,32,3584]{2,1,0:T(8,128)(2,1)} %second_ref.1) | copy-start | bytes 688132

commit v6 on v5

--- a/solution.py
+++ b/solution.py
@@ -49,6 +49,40 @@
         scratch_shapes=[pltpu.SemaphoreType.DMA((N_X, 2))],
         compiler_params=pltpu.CompilerParams(vmem_limit_bytes=KERNEL_VMEM),
     )(near)
+
+
+def unpacked(held, span, units):
+    rows = held[0].shape[0]
+
+    def kernel(*refs):
+        blocks, (columns, routed, owned), sems = refs[:N_X], refs[N_X : N_X + 3], refs[-1]
+        x = lax.axis_index("x")
+        copies = []
+        for step, block in enumerate(blocks):
+            here = lax.rem(x + N_X - step, N_X)
+            parts = (
+                (block.at[:, :span], columns.at[step]),
+                (block.at[:, span : span + units], routed.at[here]),
+                (block.at[:, span + units :], owned.at[step]),
+            )
+            for j, (source, target) in enumerate(parts):
+                copies.append(pltpu.make_async_copy(source, target, sems.at[step, j]))
+                copies[-1].start()
+        for copy in copies:
+            copy.wait()
+
+    outs = pl.pallas_call(
+        kernel,
+        out_shape=tuple(
+            jax.ShapeDtypeStruct((N_X, rows, n), held[0].dtype) for n in (span, units, units)
+        ),
+        in_specs=[pl.BlockSpec(memory_space=pl.ANY)] * N_X,
+        out_specs=(pl.BlockSpec(memory_space=pl.ANY),) * 3,
+        scratch_shapes=[pltpu.SemaphoreType.DMA((N_X, 3))],
+        compiler_params=pltpu.CompilerParams(vmem_limit_bytes=KERNEL_VMEM),
+        cost_estimate=pl.CostEstimate(flops=2 * 10**10, bytes_accessed=2**21, transcendentals=0),
+    )(*held)
+    return tuple(out.reshape(N_X * rows, -1) for out in outs)
 
 
 def adamw(sums, weight, moment, second):
@@ -112,7 +146,8 @@
     is_live = (slot_ids[None, :] < filled[:, None]).reshape(rows)
     hidden = jnp.where(is_live[:, None], hidden, jnp.zeros_like(hidden))
     hidden = hidden.reshape(-1, 2, slots, units).transpose(1, 0, 2, 3).reshape(rows, units)
-    owned_hidden = local_hidden[0, 0]
+    both = jnp.concatenate([hidden, local_hidden[0, 0]]).reshape(2, rows, -1, 2, OWNED)
+    hidden, owned_hidden = both.transpose(0, 1, 3, 2, 4).reshape(2, rows, units)
     owned_gradients = local_grads[0, 0]
 
     held = []
@@ -130,22 +165,15 @@
     gathered = lax.all_to_all(blocks, ("x", "y_low"), 0, 0, tiled=True)
     gathered = gathered.reshape(-1, span)
 
-    def by_core(rows_of_units):
-        split = rows_of_units.reshape(-1, units // (2 * OWNED), 2, OWNED)
-        return split.transpose(0, 2, 1, 3).reshape(-1, units)
-
-    back = jnp.stack([block[:, span : span + units] for block in held[::-1]])
-    twice = jnp.concatenate([back, back])
-    routed = lax.dynamic_slice_in_dim(twice, N_X - 1 - x, N_X, axis=0).reshape(-1, units)
-    routed = by_core(routed)
-    owned = by_core(jnp.concatenate([block[:, span + units :] for block in held]))
-    columns = jnp.concatenate([block[:, :span] for block in held])
+    columns, routed, owned = unpacked(held, span, units)
+
+    local = contract_rows(owned, columns)
 
     def partial_of(which):
         start = which * share
-        return contract_rows(
-            lax.dynamic_slice_in_dim(owned, start, share, axis=1), columns
-        ) + contract_rows(lax.dynamic_slice_in_dim(routed, start, share, axis=1), gathered)
+        return lax.dynamic_slice_in_dim(local, start, share, axis=0) + contract_rows(
+            lax.dynamic_slice_in_dim(routed, start, share, axis=1), gathered
+        )
 
     other = partial_of(1 - core).astype(jnp.bfloat16)
     other = lax.ppermute(other, "core", [(0, 1), (1, 0)])

time: 101 us -> 102 us (level)
  waiting for transfers between devices: 22.8 us -> 27.5 us
  local copies, waits for them, and re-layouts: 6.34 us -> 2.61 us
    all_to_all x1, waiting for transfers between devices: 6.65 us -> 11.1 us  [on_device(): gathered = lax.all_to_all(blocks, ('x', 'y_low'), 0, 0, tiled=True)]
    slice x8 -> x0, local copies, waits for them, and re-layouts: 2.87 us -> none  [the longest x4 2.83 us: on_device(): columns = jnp.concatenate([block[:, :span] for block in held])]
    ppermute x1, waiting for transfers between devices: 0.02 us -> 2.08 us  [on_device(): other = lax.ppermute(other, 'core', [(0, 1), (1, 0)])]
    all_to_all x1, waiting for transfers between devices: 16.1 us -> 14.4 us  [on_device(): arrived = lax.all_to_all(outgoing, ('z', 'y_half'), 0, 0, tiled=True)]
    unnamed x30 -> x12, local copies, waits for them, and re-layouts: 1.33 us -> 0.12 us
    dot_general x4 -> x3, matrix products: 3.09 us -> 3.45 us  [contract_rows(): lax.dot_general(left_rows, right_rows, (((0,), (0,)), ((), ())), preferre...]
  transfers between devices with their start and end apart: 6 -> 6, of which waited for: 2 -> 3; matrix products, arithmetic and copies ran while one was open for 9% -> 5% of each run, Pallas kernels for 1% -> 1%
where the time goes in v6:
time: 102 us
  starting transfers between devices  40 us (39%)
  waiting for transfers between devices  27.5 us (27%)
  blocking collectives  23.2 us (23%)
  matrix products  3.45 us (3%)
  local copies, waits for them, and re-layouts  2.61 us (3%)
  Pallas kernels  2.57 us (3%)
  other arithmetic  1.55 us (2%)
    all_to_all x1, blocking collectives, on_device(): partial = lax.all_to_all(partial, ('y_hi', 'x'), 0, 0, tiled=True)  23.2 us
    all_to_all x1, starting transfers between devices, on_device(): arrived = lax.all_to_all(outgoing, ('z', 'y_half'), 0, 0, tiled=True)  21.4 us
    all_to_all x1, waiting for transfers between devices, on_device(): arrived = lax.all_to_all(outgoing, ('z', 'y_half'), 0, 0, tiled=True)  14.4 us
    ppermute x3, starting transfers between devices, on_device(): lax.ppermute(held[step], 'x', [(i, (i + step) % N_X) for i in range(N_X)])  11.4 us
    all_to_all x1, waiting for transfers between devices, on_device(): gathered = lax.all_to_all(blocks, ('x', 'y_low'), 0, 0, tiled=True)  11.1 us
    all_to_all x1, starting transfers between devices, on_device(): gathered = lax.all_to_all(blocks, ('x', 'y_low'), 0, 0, tiled=True)  5.32 us
    dot_general x3, matrix products, contract_rows(): lax.dot_general(left_rows, right_rows, (((0,), (0,)), ((), ())), preferre...  3.45 us
    ppermute x1, waiting for transfers between devices, on_device(): other = lax.ppermute(other, 'core', [(0, 1), (1, 0)])  2.08 us
  transfers between devices with their start and end apart: 6, of which 3 were waited for; matrix products, arithmetic and copies ran while one was open for 5% of the time, Pallas kernels for 1%

profile of v6, /device:TPU:16, one launch (start us, length us, event | category | flops | bytes accessed | tf_op | source)
XLA Modules:
  0.0 101.8 jit_solution(9560051999847692567)
XLA Ops:
  0.7 21.4 %all-to-all-start = ((bf16[32,2,3584]{2,1,0:T(2,128)(2,1)}), bf16[32,2,3584]{2,1,0:T(2,128)(2,1)S(1)}, u32[]{:S(2)}, u32[]{:S(2)}) async-start(bf16[32,2,3584]{2,1,0:T(2,128)(2,1)} %bitcast.36), calls=%async_computation | async-start | bytes 917504 | tf_op jit(solution)/shard_map/all_to_all | solution.py:142
  22.3 1.0 squeeze.13
  23.4 0.2 fusion.3
  23.7 0.1 copy.17
  23.9 0.5 fusion.7
  24.5 0.1 copy.20
  24.7 0.1 copy.21
  25.0 1.3 %pad_maximum_fusion = (bf16[128,1920]{1,0:T(8,128)(2,1)}, bf16[128,1920]{1,0:T(8,128)(2,1)}, bf16[128,1920]{1,0:T(8,128)(2,1)}, bf16[128,1920]{1,0:T(8,128)(2,1)S(1)}) fusion(bf16[128,512]{1,0:T(8,128)(2,1)S(1)} %copy.21, bf16[128,512]{1,0:T(8,128)(2,1)S(1)} %copy.20, bf16[128,896]{1,0:T(8,128)(2,1)S(1)} %get-tuple-element.17, ...), kind=kLoop, calls=%fused_computation.5 | loop fusion | flops 4423680 | bytes 3145728 | tf_op jit(solution)/shard_map/concatenate | solution.py:157
  26.2 3.4 %collective-permute-start = (bf16[128,1920]{1,0:T(8,128)(2,1)}, bf16[128,1920]{1,0:T(8,128)(2,1)S(1)}, u32[]{:S(2)}, u32[]{:S(2)}) collective-permute-start(bf16[128,1920]{1,0:T(8,128)(2,1)} %get-tuple-element.22), channel_id=1, source_target_pairs={{0,128},{128,256},{256,384},{384,0},{1,129},{129,257},{257,385},{3... | collective-permute-start | bytes 1474568 | tf_op jit(solution)/shard_map/ppermute | solution.py:159
  29.6 4.6 %collective-permute-start.1 = (bf16[128,1920]{1,0:T(8,128)(2,1)}, bf16[128,1920]{1,0:T(8,128)(2,1)S(1)}, u32[]{:S(2)}, u32[]{:S(2)}) collective-permute-start(bf16[128,1920]{1,0:T(8,128)(2,1)} %get-tuple-element.23), channel_id=1, source_target_pairs={{0,256},{128,384},{256,0},{384,128},{1,257},{129,385},{257,1},{385... | collective-permute-start | bytes 1474568 | tf_op jit(solution)/shard_map/ppermute | solution.py:159
  34.3 3.3 %collective-permute-start.2 = (bf16[128,1920]{1,0:T(8,128)(2,1)}, bf16[128,1920]{1,0:T(8,128)(2,1)S(1)}, u32[]{:S(2)}, u32[]{:S(2)}) collective-permute-start(bf16[128,1920]{1,0:T(8,128)(2,1)} %get-tuple-element.21), channel_id=1, source_target_pairs={{0,384},{128,0},{256,128},{384,256},{1,385},{129,1},{257,129},{385... | collective-permute-start | bytes 1474568 | tf_op jit(solution)/shard_map/ppermute | solution.py:159
  37.6 14.4 %all-to-all-done = bf16[32,2,3584]{2,1,0:T(2,128)(2,1)S(1)} async-done(((bf16[32,2,3584]{2,1,0:T(2,128)(2,1)}), bf16[32,2,3584]{2,1,0:T(2,128)(2,1)S(1)}, u32[]{:S(2)}, u32[]{:S(2)}) %all-to-all-start) | async-done | bytes 458784 | tf_op jit(solution)/shard_map/all_to_all | solution.py:142
  52.0 0.2 reshape.64.near_ref
  52.2 1.0 shard_map.103
  53.2 5.3 %all-to-all-start.1 = ((bf16[8,64,896]{2,1,0:T(8,128)(2,1)}), bf16[8,64,896]{2,1,0:T(8,128)(2,1)S(1)}, u32[]{:S(2)}, u32[]{:S(2)}) async-start(bf16[8,64,896]{2,1,0:T(8,128)(2,1)} %shard_map.103), calls=%async_computation.1 | async-start | bytes 1835008 | tf_op jit(solution)/shard_map/all_to_all | solution.py:165
  58.5 0.3 shard_map.104
  58.9 0.7 convolution_bitcast_fusion
  59.6 11.1 %all-to-all-done.1 = bf16[8,64,896]{2,1,0:T(8,128)(2,1)S(1)} async-done(((bf16[8,64,896]{2,1,0:T(8,128)(2,1)}), bf16[8,64,896]{2,1,0:T(8,128)(2,1)S(1)}, u32[]{:S(2)}, u32[]{:S(2)}) %all-to-all-start.1) | async-done | bytes 917536 | tf_op jit(solution)/shard_map/all_to_all | solution.py:165
  70.7 1.2 %fusion = bf16[256,896]{1,0:T(8,128)(2,1)} fusion(bf16[512,896]{1,0:T(8,128)(2,1)S(1)} %bitcast.30, f32[512,896]{1,0:T(8,128)S(1)} %convolution_bitcast_fusion, s32[]{:T(128)S(6)} %select_n.36, bf16[512,512]{1,0:T(8,128)(2,1)S(1)} %bitcast.28), kind=kOutput, calls=%fused_computation.3 | convolution fusion | flops 235339776 | bytes 2556928 | tf_op jit(solution)/shard_map/dot_general | solution.py:23
  71.9 1.9 %collective-permute-start.3 = (bf16[256,896]{1,0:T(8,128)(2,1)}, bf16[256,896]{1,0:T(8,128)(2,1)}, u32[]{:S(2)}, u32[]{:S(2)}) collective-permute-start(bf16[256,896]{1,0:T(8,128)(2,1)} %fusion), channel_id=1, source_target_pairs={{0,64},{64,0},{1,65},{65,1},{2,66},{66,2},{3,67},{67,3},{4,68},{68... | collective-permute-start | bytes 1376264 | tf_op jit(solution)/shard_map/ppermute | solution.py:179
  73.9 2.1 %collective-permute-done.3 = bf16[256,896]{1,0:T(8,128)(2,1)} collective-permute-done((bf16[256,896]{1,0:T(8,128)(2,1)}, bf16[256,896]{1,0:T(8,128)(2,1)}, u32[]{:S(2)}, u32[]{:S(2)}) %collective-permute-start.3) | collective-permute-done | bytes 458784 | tf_op jit(solution)/shard_map/ppermute | solution.py:179
  75.9 1.5 %add_convert_fusion = bf16[256,896]{1,0:T(8,128)(2,1)S(1)} fusion(bf16[256,896]{1,0:T(8,128)(2,1)} %collective-permute-done.3, bf16[512,896]{1,0:T(8,128)(2,1)S(1)} %bitcast.31, f32[512,896]{1,0:T(8,128)S(1)} %convolution_bitcast_fusion, s32[]{:T(128)S(6)} %select_n.35, bf16[512,512]{1,0:T(8,128)(2,1)S(1)} %bitcast.29), kind=kOutput, calls=%fused_computation.4 | convolution fusion | flops 235798528 | bytes 3015680 | tf_op jit(solution)/shard_map/dot_general | solution.py:23
  77.4 23.2 %all_to_all.15.sums_ref = bf16[8,32,896]{2,1,0:T(8,128)(2,1)S(1)} all-to-all(bf16[8,32,896]{2,1,0:T(8,128)(2,1)S(1)} %bitcast.33), channel_id=1, replica_groups=mesh['y_hi'=2,'x'=4,'core'=2,'z'=16,'y_half'=2,'y_low'=2] {'y_hi','x'}, dimensions={0} | all-to-all | bytes 917504 | tf_op jit(solution)/shard_map/all_to_all | solution.py:183
  100.6 1.2 %shard_map.105 = (f32[1,32,3584]{2,1,0:T(8,128)}, bf16[1,32,3584]{2,1,0:T(8,128)(2,1)}, bf16[1,32,3584]{2,1,0:T(8,128)(2,1)}) custom-call(bf16[8,32,896]{2,1,0:T(8,128)(2,1)S(1)} %all_to_all.15.sums_ref, f32[1,32,3584]{2,1,0:T(8,128)S(1)} %copy-done.1, bf16[1,32,3584]{2,1,0:T(8,128)(2,1)S(1)} %copy-done.2, bf16[1,32,3584]{2,1,0:T(8,128)(2,1)S(1)} %copy-done.3), custom_call_target="tpu_custom_call" | custom-call | tf_op jit(solution)/shard_map/pallas_call | solution.py:118
  (25 shorter events, 0.7 us)
Async XLA Ops:
  0.6 21.5 %copy-start = (s32[1,64,32]{1,2,0:T(8,128)S(1)}, s32[1,64,32]{1,2,0:T(8,128)}, u32[]{:S(2)}) copy-start(s32[1,64,32]{1,2,0:T(8,128)} %param.12) | copy-start | bytes 24580
  0.6 23.0 %copy-start.5 = (bf16[1,1,128,512]{3,2,1,0:T(8,128)(2,1)S(1)}, bf16[1,1,128,512]{3,2,1,0:T(8,128)(2,1)}, u32[]{:S(2)}) copy-start(bf16[1,1,128,512]{3,2,1,0:T(8,128)(2,1)} %param.10) | copy-start | bytes 393220
  0.7 51.3 %all-to-all-start = ((bf16[32,2,3584]{2,1,0:T(2,128)(2,1)}), bf16[32,2,3584]{2,1,0:T(2,128)(2,1)S(1)}, u32[]{:S(2)}, u32[]{:S(2)}) async-start(bf16[32,2,3584]{2,1,0:T(2,128)(2,1)} %bitcast.36), calls=%async_computation | async-start | bytes 917504 | tf_op jit(solution)/shard_map/all_to_all | solution.py:142
  23.7 1.2 %copy-start.4 = (bf16[1,1,128,3584]{3,2,1,0:T(8,128)(2,1)S(1)}, bf16[1,1,128,3584]{3,2,1,0:T(8,128)(2,1)}, u32[]{:S(2)}) copy-start(bf16[1,1,128,3584]{3,2,1,0:T(8,128)(2,1)} %param.11) | copy-start | bytes 2752516
  26.2 32.3 %collective-permute-start = (bf16[128,1920]{1,0:T(8,128)(2,1)}, bf16[128,1920]{1,0:T(8,128)(2,1)S(1)}, u32[]{:S(2)}, u32[]{:S(2)}) collective-permute-start(bf16[128,1920]{1,0:T(8,128)(2,1)} %get-tuple-element.22), channel_id=1, source_target_pairs={{0,128},{128,256},{256,384},{384,0},{1,129},{129,257},{257,385},{3... | collective-permute-start | bytes 1474568 | tf_op jit(solution)/shard_map/ppermute | solution.py:159
  29.6 28.9 %collective-permute-start.1 = (bf16[128,1920]{1,0:T(8,128)(2,1)}, bf16[128,1920]{1,0:T(8,128)(2,1)S(1)}, u32[]{:S(2)}, u32[]{:S(2)}) collective-permute-start(bf16[128,1920]{1,0:T(8,128)(2,1)} %get-tuple-element.23), channel_id=1, source_target_pairs={{0,256},{128,384},{256,0},{384,128},{1,257},{129,385},{257,1},{385... | collective-permute-start | bytes 1474568 | tf_op jit(solution)/shard_map/ppermute | solution.py:159
  34.3 24.3 %collective-permute-start.2 = (bf16[128,1920]{1,0:T(8,128)(2,1)}, bf16[128,1920]{1,0:T(8,128)(2,1)S(1)}, u32[]{:S(2)}, u32[]{:S(2)}) collective-permute-start(bf16[128,1920]{1,0:T(8,128)(2,1)} %get-tuple-element.21), channel_id=1, source_target_pairs={{0,384},{128,0},{256,128},{384,256},{1,385},{129,1},{257,129},{385... | collective-permute-start | bytes 1474568 | tf_op jit(solution)/shard_map/ppermute | solution.py:159
  53.2 17.5 %all-to-all-start.1 = ((bf16[8,64,896]{2,1,0:T(8,128)(2,1)}), bf16[8,64,896]{2,1,0:T(8,128)(2,1)S(1)}, u32[]{:S(2)}, u32[]{:S(2)}) async-start(bf16[8,64,896]{2,1,0:T(8,128)(2,1)} %shard_map.103), calls=%async_computation.1 | async-start | bytes 1835008 | tf_op jit(solution)/shard_map/all_to_all | solution.py:165
  71.9 4.0 %collective-permute-start.3 = (bf16[256,896]{1,0:T(8,128)(2,1)}, bf16[256,896]{1,0:T(8,128)(2,1)}, u32[]{:S(2)}, u32[]{:S(2)}) collective-permute-start(bf16[256,896]{1,0:T(8,128)(2,1)} %fusion), channel_id=1, source_target_pairs={{0,64},{64,0},{1,65},{65,1},{2,66},{66,2},{3,67},{67,3},{4,68},{68... | collective-permute-start | bytes 1376264 | tf_op jit(solution)/shard_map/ppermute | solution.py:179
  73.8 26.8 %copy-start.1 = (f32[1,32,3584]{2,1,0:T(8,128)S(1)}, f32[1,32,3584]{2,1,0:T(8,128)}, u32[]{:S(2)}) copy-start(f32[1,32,3584]{2,1,0:T(8,128)} %weight_ref.1) | copy-start | bytes 1376260
  73.8 26.8 %copy-start.2 = (bf16[1,32,3584]{2,1,0:T(8,128)(2,1)S(1)}, bf16[1,32,3584]{2,1,0:T(8,128)(2,1)}, u32[]{:S(2)}) copy-start(bf16[1,32,3584]{2,1,0:T(8,128)(2,1)} %moment_ref.1) | copy-start | bytes 688132
  73.8 26.8 %copy-start.3 = (bf16[1,32,3584]{2,1,0:T(8,128)(2,1)S(1)}, bf16[1,32,3584]{2,1,0:T(8,128)(2,1)}, u32[]{:S(2)}) copy-start(bf16[1,32,3584]{2,1,0:T(8,128)(2,1)} %second_ref.1) | copy-start | bytes 688132

commit v7 on v6

--- a/solution.py
+++ b/solution.py
@@ -5,7 +5,7 @@
 from jax.experimental.pallas import tpu as pltpu
 from jax.sharding import Mesh, PartitionSpec as P
 
-AXES = ("y_hi", "x", "core", "z", "y_half", "y_low")
+AXES = ("y_hi", "x", "core", "z_hi", "z_lo", "y_half", "y_low")
 N_X = 4
 OWNED = 32
 KERNEL_VMEM = 8 * 2**20
@@ -26,27 +26,20 @@
 
 
 def column_blocks(near, span):
-    rows = near.shape[0]
-
-    def kernel(near_ref, out_ref, sems):
-        copies = [
-            pltpu.make_async_copy(
-                near_ref.at[:, i * span : (i + 1) * span], out_ref.at[2 * i + j], sems.at[i, j]
-            )
-            for i in range(N_X)
-            for j in range(2)
-        ]
-        for copy in copies:
-            copy.start()
-        for copy in copies:
-            copy.wait()
+    rows = near.shape[1]
+
+    def kernel(near_ref, out_ref):
+        for i in range(N_X):
+            for k in range(2):
+                block = near_ref[k, :, i * span : (i + 1) * span]
+                for j in range(2):
+                    out_ref[4 * i + 2 * k + j] = block
 
     return pl.pallas_call(
         kernel,
-        out_shape=jax.ShapeDtypeStruct((2 * N_X, rows, span), near.dtype),
+        out_shape=jax.ShapeDtypeStruct((4 * N_X, rows, span), near.dtype),
         in_specs=[pl.BlockSpec(memory_space=pltpu.VMEM)],
-        out_specs=pl.BlockSpec(memory_space=pl.ANY),
-        scratch_shapes=[pltpu.SemaphoreType.DMA((N_X, 2))],
+        out_specs=pl.BlockSpec(memory_space=pltpu.VMEM),
         compiler_params=pltpu.CompilerParams(vmem_limit_bytes=KERNEL_VMEM),
     )(near)
 
@@ -80,7 +73,7 @@
         out_specs=(pl.BlockSpec(memory_space=pl.ANY),) * 3,
         scratch_shapes=[pltpu.SemaphoreType.DMA((N_X, 3))],
         compiler_params=pltpu.CompilerParams(vmem_limit_bytes=KERNEL_VMEM),
-        cost_estimate=pl.CostEstimate(flops=2 * 10**10, bytes_accessed=2**21, transcendentals=0),
+        cost_estimate=pl.CostEstimate(flops=6 * 10**10, bytes_accessed=2**21, transcendentals=0),
     )(*held)
     return tuple(out.reshape(N_X * rows, -1) for out in outs)
 
@@ -131,7 +124,7 @@
 ):
     x = lax.axis_index("x")
     core = lax.axis_index("core")
-    expert_id = lax.axis_index("z") * 2 + lax.axis_index("y_half")
+    expert_id = lax.axis_index(("z_hi", "z_lo", "y_half"))
     outgoing = token_gradients[0, 0]
     slots, features = outgoing.shape[1:]
     hidden = hidden_acts[0, 0]
@@ -139,13 +132,16 @@
     span = features // N_X
     share = units // 2
 
-    arrived = lax.all_to_all(outgoing, ("z", "y_half"), 0, 0, tiled=True)
+    outgoing = outgoing.reshape(-1, 2, 2, slots, features).transpose(0, 2, 1, 3, 4)
+    outgoing = outgoing.reshape(-1, 2, slots, features)
+    arrived = lax.all_to_all(outgoing, ("z_hi", "y_half"), 0, 0, tiled=True)
 
     filled = lax.dynamic_index_in_dim(counts[0], expert_id, axis=1, keepdims=False)
     slot_ids = jnp.arange(slots, dtype=jnp.int32)
     is_live = (slot_ids[None, :] < filled[:, None]).reshape(rows)
     hidden = jnp.where(is_live[:, None], hidden, jnp.zeros_like(hidden))
-    hidden = hidden.reshape(-1, 2, slots, units).transpose(1, 0, 2, 3).reshape(rows, units)
+    hidden = hidden.reshape(-1, 2, 2, 2, slots, units).transpose(1, 3, 0, 2, 4, 5)
+    hidden = hidden.reshape(rows, units)
     both = jnp.concatenate([hidden, local_hidden[0, 0]]).reshape(2, rows, -1, 2, OWNED)
     hidden, owned_hidden = both.transpose(0, 1, 3, 2, 4).reshape(2, rows, units)
     owned_gradients = local_grads[0, 0]
@@ -160,20 +156,19 @@
             held[step], "x", [(i, (i + step) % N_X) for i in range(N_X)]
         )
 
-    blocks = column_blocks(arrived.reshape(-1, features), span)
+    near = arrived.transpose(1, 0, 2, 3).reshape(2, -1, features)
+    blocks = column_blocks(near, span)
     held, _ = lax.optimization_barrier((held, blocks))
-    gathered = lax.all_to_all(blocks, ("x", "y_low"), 0, 0, tiled=True)
+    gathered = lax.all_to_all(blocks, ("x", "z_lo", "y_low"), 0, 0, tiled=True)
     gathered = gathered.reshape(-1, span)
 
     columns, routed, owned = unpacked(held, span, units)
-
-    local = contract_rows(owned, columns)
 
     def partial_of(which):
         start = which * share
-        return lax.dynamic_slice_in_dim(local, start, share, axis=0) + contract_rows(
-            lax.dynamic_slice_in_dim(routed, start, share, axis=1), gathered
-        )
+        return contract_rows(
+            lax.dynamic_slice_in_dim(owned, start, share, axis=1), columns
+        ) + contract_rows(lax.dynamic_slice_in_dim(routed, start, share, axis=1), gathered)
 
     other = partial_of(1 - core).astype(jnp.bfloat16)
     other = lax.ppermute(other, "core", [(0, 1), (1, 0)])
@@ -186,8 +181,8 @@
 
 def solution(mesh):
     dp = ("y_hi", "x", "core")
-    expert = ("z", "y_half", "y_low")
-    fine = Mesh(mesh.devices.reshape(2, N_X, 2, 16, 2, 2), AXES)
+    expert = ("z_hi", "z_lo", "y_half", "y_low")
+    fine = Mesh(mesh.devices.reshape(2, N_X, 2, 8, 2, 2, 2), AXES)
     outs = P(expert, dp, None)
     return jax.shard_map(
         on_device,

time: 102 us -> 106 us (1.039)
  the two profiles are of different devices: /device:TPU:16 before, /device:TPU:8 now
where the time goes in v7:
time: 106 us; the launch traced here: 105 us
  starting transfers between devices  43.2 us (41%)
  blocking collectives  22.7 us (21%)
  waiting for transfers between devices  21.6 us (20%)
  local copies, waits for them, and re-layouts  8.18 us (8%)
  matrix products  4.23 us (4%)
  Pallas kernels  2.61 us (2%)
  other arithmetic  1.58 us (1%)
    all_to_all x1, blocking collectives, on_device(): partial = lax.all_to_all(partial, ('y_hi', 'x'), 0, 0, tiled=True)  22.7 us
    all_to_all x1, starting transfers between devices, on_device(): arrived = lax.all_to_all(outgoing, ('z_hi', 'y_half'), 0, 0, tiled=True)  20.9 us
    ppermute x3, starting transfers between devices, on_device(): lax.ppermute(held[step], 'x', [(i, (i + step) % N_X) for i in range(N_X)])  11.4 us
    all_to_all x1, waiting for transfers between devices, on_device(): gathered = lax.all_to_all(blocks, ('x', 'z_lo', 'y_low'), 0, 0, tiled=True)  11.3 us
    all_to_all x1, starting transfers between devices, on_device(): gathered = lax.all_to_all(blocks, ('x', 'z_lo', 'y_low'), 0, 0, tiled=True)  9.03 us
    all_to_all x1, waiting for transfers between devices, on_device(): arrived = lax.all_to_all(outgoing, ('z_hi', 'y_half'), 0, 0, tiled=True)  8.99 us
    dot_general x4, matrix products, contract_rows(): lax.dot_general(left_rows, right_rows, (((0,), (0,)), ((), ())), preferre...  4.23 us
    unnamed x18, local copies, waits for them, and re-layouts  4.04 us
  transfers between devices with their start and end apart: 6, of which 3 were waited for; matrix products, arithmetic and copies ran while one was open for 4% of the time, Pallas kernels for 1%

profile of v7, /device:TPU:8, one launch (start us, length us, event | category | flops | bytes accessed | tf_op | source)
XLA Modules:
  0.0 105.1 jit_solution(16236177358288181136)
XLA Ops:
  0.6 2.1 %copy.42 = bf16[8,2,2,2,3584]{4,3,1,2,0:T(2,128)(2,1)} copy(bf16[8,2,2,2,3584]{4,3,2,1,0:T(2,128)(2,1)} %bitcast.43) | data formatting | bytes 917504 | tf_op jit(solution)/shard_map/reshape;squeeze | solution.py:135
  2.8 20.9 %all-to-all-start = ((bf16[16,2,2,3584]{3,2,1,0:T(2,128)(2,1)}), bf16[16,2,2,3584]{3,2,1,0:T(2,128)(2,1)S(1)}, u32[]{:S(2)}, u32[]{:S(2)}) async-start(bf16[16,2,2,3584]{3,2,1,0:T(2,128)(2,1)} %bitcast.11), calls=%async_computation | async-start | bytes 917504 | tf_op jit(solution)/shard_map/all_to_all | solution.py:137
  24.0 0.5 copy-done.7
  25.0 0.8 copy-done.8
  26.1 0.5 fusion.15
  27.0 0.9 copy-done.6
  27.9 1.3 %pad_maximum_fusion = (bf16[128,1920]{1,0:T(8,128)(2,1)}, bf16[128,1920]{1,0:T(8,128)(2,1)}, bf16[128,1920]{1,0:T(8,128)(2,1)}, bf16[128,1920]{1,0:T(8,128)(2,1)S(1)}) fusion(bf16[128,512]{1,0:T(8,128)(2,1)S(1)} %copy.35, bf16[128,512]{1,0:T(8,128)(2,1)S(1)} %copy.34, bf16[128,896]{1,0:T(8,128)(2,1)S(1)} %get-tuple-element.17, ...), kind=kLoop, calls=%fused_computation.4 | loop fusion | flops 4423680 | bytes 3145728 | tf_op jit(solution)/shard_map/concatenate | solution.py:153
  29.1 3.4 %collective-permute-start = (bf16[128,1920]{1,0:T(8,128)(2,1)}, bf16[128,1920]{1,0:T(8,128)(2,1)S(1)}, u32[]{:S(2)}, u32[]{:S(2)}) collective-permute-start(bf16[128,1920]{1,0:T(8,128)(2,1)} %get-tuple-element.22), channel_id=1, source_target_pairs={{0,128},{128,256},{256,384},{384,0},{1,129},{129,257},{257,385},{3... | collective-permute-start | bytes 1474568 | tf_op jit(solution)/shard_map/ppermute | solution.py:155
  32.5 4.6 %collective-permute-start.1 = (bf16[128,1920]{1,0:T(8,128)(2,1)}, bf16[128,1920]{1,0:T(8,128)(2,1)S(1)}, u32[]{:S(2)}, u32[]{:S(2)}) collective-permute-start(bf16[128,1920]{1,0:T(8,128)(2,1)} %get-tuple-element.23), channel_id=1, source_target_pairs={{0,256},{128,384},{256,0},{384,128},{1,257},{129,385},{257,1},{385... | collective-permute-start | bytes 1474568 | tf_op jit(solution)/shard_map/ppermute | solution.py:155
  37.2 3.3 %collective-permute-start.2 = (bf16[128,1920]{1,0:T(8,128)(2,1)}, bf16[128,1920]{1,0:T(8,128)(2,1)S(1)}, u32[]{:S(2)}, u32[]{:S(2)}) collective-permute-start(bf16[128,1920]{1,0:T(8,128)(2,1)} %get-tuple-element.21), channel_id=1, source_target_pairs={{0,384},{128,0},{256,128},{384,256},{1,385},{129,1},{257,129},{385... | collective-permute-start | bytes 1474568 | tf_op jit(solution)/shard_map/ppermute | solution.py:155
  40.5 9.0 %all-to-all-done = bf16[16,2,2,3584]{3,2,1,0:T(2,128)(2,1)S(1)} async-done(((bf16[16,2,2,3584]{3,2,1,0:T(2,128)(2,1)}), bf16[16,2,2,3584]{3,2,1,0:T(2,128)(2,1)S(1)}, u32[]{:S(2)}, u32[]{:S(2)}) %all-to-all-start) | async-done | bytes 458784 | tf_op jit(solution)/shard_map/all_to_all | solution.py:137
  50.0 1.1 %shard_map.103 = bf16[16,32,896]{2,1,0:T(8,128)(2,1)} custom-call(bf16[2,32,3584]{2,1,0:T(8,128)(2,1)S(1)} %reshape.72.near_ref), custom_call_target="tpu_custom_call" | custom-call | tf_op jit(solution)/shard_map/pallas_call | solution.py:38
  51.1 9.0 %all-to-all-start.1 = ((bf16[16,32,896]{2,1,0:T(8,128)(2,1)}), bf16[16,32,896]{2,1,0:T(8,128)(2,1)}, u32[]{:S(2)}, u32[]{:S(2)}) async-start(bf16[16,32,896]{2,1,0:T(8,128)(2,1)} %shard_map.103), calls=%async_computation.1 | async-start | bytes 1835008 | tf_op jit(solution)/shard_map/all_to_all | solution.py:162
  60.1 0.8 copy-done.4
  60.9 1.0 copy-done.5
  62.3 0.5 fusion.2
  62.8 11.3 %all-to-all-done.1 = bf16[16,32,896]{2,1,0:T(8,128)(2,1)} async-done(((bf16[16,32,896]{2,1,0:T(8,128)(2,1)}), bf16[16,32,896]{2,1,0:T(8,128)(2,1)}, u32[]{:S(2)}, u32[]{:S(2)}) %all-to-all-start.1) | async-done | bytes 917536 | tf_op jit(solution)/shard_map/all_to_all | solution.py:162
  74.1 1.6 %fusion = bf16[256,896]{1,0:T(8,128)(2,1)S(1)} fusion(f32[256,896]{1,0:T(8,128)S(1)} %fusion.2, bf16[512,896]{1,0:T(8,128)(2,1)} %bitcast.16, bf16[512,512]{1,0:T(8,128)(2,1)S(1)} %bitcast.36, s32[]{:T(128)S(6)} %select_n.36), kind=kOutput, calls=%fused_computation.2 | convolution fusion | flops 235339776 | bytes 2555908 | tf_op jit(solution)/shard_map/dot_general | solution.py:23
  75.7 1.9 %collective-permute-start.3 = (bf16[256,896]{1,0:T(8,128)(2,1)S(1)}, bf16[256,896]{1,0:T(8,128)(2,1)S(1)}, u32[]{:S(2)}, u32[]{:S(2)}) collective-permute-start(bf16[256,896]{1,0:T(8,128)(2,1)S(1)} %fusion), channel_id=1, source_target_pairs={{0,64},{64,0},{1,65},{65,1},{2,66},{66,2},{3,67},{67,3},{4,68},{68... | collective-permute-start | bytes 1376264 | tf_op jit(solution)/shard_map/ppermute | solution.py:174
  77.7 0.5 fusion.7
  78.1 1.3 %collective-permute-done.3 = bf16[256,896]{1,0:T(8,128)(2,1)S(1)} collective-permute-done((bf16[256,896]{1,0:T(8,128)(2,1)S(1)}, bf16[256,896]{1,0:T(8,128)(2,1)S(1)}, u32[]{:S(2)}, u32[]{:S(2)}) %collective-permute-start.3) | collective-permute-done | bytes 458784 | tf_op jit(solution)/shard_map/ppermute | solution.py:174
  79.5 1.6 %add_convert_fusion = bf16[256,896]{1,0:T(8,128)(2,1)S(1)} fusion(bf16[256,896]{1,0:T(8,128)(2,1)S(1)} %collective-permute-done.3, f32[256,896]{1,0:T(8,128)S(1)} %fusion.7, bf16[512,896]{1,0:T(8,128)(2,1)} %bitcast.16, bf16[512,512]{1,0:T(8,128)(2,1)S(1)} %bitcast.37, s32[]{:T(128)S(6)} %select_n.35), kind=kOutput, calls=%fused_computation.3 | convolution fusion | flops 235798528 | bytes 3014660 | tf_op jit(solution)/shard_map/dot_general | solution.py:23
  81.1 22.7 %all_to_all.15.sums_ref = bf16[8,32,896]{2,1,0:T(8,128)(2,1)S(1)} all-to-all(bf16[8,32,896]{2,1,0:T(8,128)(2,1)S(1)} %bitcast.39), channel_id=1, replica_groups=mesh['y_hi'=2,'x'=4,'core'=2,'z_hi'=8,'z_lo'=2,'y_half'=2,'y_low'=2] {'y..., dimensions={0} | all-to-all | bytes 917504 | tf_op jit(solution)/shard_map/all_to_all | solution.py:178
  103.8 1.2 %shard_map.105 = (f32[1,32,3584]{2,1,0:T(8,128)}, bf16[1,32,3584]{2,1,0:T(8,128)(2,1)}, bf16[1,32,3584]{2,1,0:T(8,128)(2,1)}) custom-call(bf16[8,32,896]{2,1,0:T(8,128)(2,1)S(1)} %all_to_all.15.sums_ref, f32[1,32,3584]{2,1,0:T(8,128)S(1)} %copy-done.1, bf16[1,32,3584]{2,1,0:T(8,128)(2,1)S(1)} %copy-done.2, bf16[1,32,3584]{2,1,0:T(8,128)(2,1)S(1)} %copy-done.3), custom_call_target="tpu_custom_call" | custom-call | tf_op jit(solution)/shard_map/pallas_call | solution.py:111
  (34 shorter events, 2.2 us)
Async XLA Ops:
  0.6 23.1 %copy-start = (s32[1,64,32]{1,2,0:T(8,128)S(1)}, s32[1,64,32]{1,2,0:T(8,128)}, u32[]{:S(2)}) copy-start(s32[1,64,32]{1,2,0:T(8,128)} %param.12) | copy-start | bytes 24580
  2.8 46.8 %all-to-all-start = ((bf16[16,2,2,3584]{3,2,1,0:T(2,128)(2,1)}), bf16[16,2,2,3584]{3,2,1,0:T(2,128)(2,1)S(1)}, u32[]{:S(2)}, u32[]{:S(2)}) async-start(bf16[16,2,2,3584]{3,2,1,0:T(2,128)(2,1)} %bitcast.11), calls=%async_computation | async-start | bytes 917504 | tf_op jit(solution)/shard_map/all_to_all | solution.py:137
  23.6 0.9 copy-start.7
  24.9 0.9 copy-start.8
  26.6 1.2 %copy-start.6 = (bf16[1,1,128,3584]{3,2,1,0:T(8,128)(2,1)S(1)}, bf16[1,1,128,3584]{3,2,1,0:T(8,128)(2,1)}, u32[]{:S(2)}) copy-start(bf16[1,1,128,3584]{3,2,1,0:T(8,128)(2,1)} %param.11) | copy-start | bytes 2752516
  29.1 31.0 %collective-permute-start = (bf16[128,1920]{1,0:T(8,128)(2,1)}, bf16[128,1920]{1,0:T(8,128)(2,1)S(1)}, u32[]{:S(2)}, u32[]{:S(2)}) collective-permute-start(bf16[128,1920]{1,0:T(8,128)(2,1)} %get-tuple-element.22), channel_id=1, source_target_pairs={{0,128},{128,256},{256,384},{384,0},{1,129},{129,257},{257,385},{3... | collective-permute-start | bytes 1474568 | tf_op jit(solution)/shard_map/ppermute | solution.py:155
  32.5 27.6 %collective-permute-start.1 = (bf16[128,1920]{1,0:T(8,128)(2,1)}, bf16[128,1920]{1,0:T(8,128)(2,1)S(1)}, u32[]{:S(2)}, u32[]{:S(2)}) collective-permute-start(bf16[128,1920]{1,0:T(8,128)(2,1)} %get-tuple-element.23), channel_id=1, source_target_pairs={{0,256},{128,384},{256,0},{384,128},{1,257},{129,385},{257,1},{385... | collective-permute-start | bytes 1474568 | tf_op jit(solution)/shard_map/ppermute | solution.py:155
  37.2 22.9 %collective-permute-start.2 = (bf16[128,1920]{1,0:T(8,128)(2,1)}, bf16[128,1920]{1,0:T(8,128)(2,1)S(1)}, u32[]{:S(2)}, u32[]{:S(2)}) collective-permute-start(bf16[128,1920]{1,0:T(8,128)(2,1)} %get-tuple-element.21), channel_id=1, source_target_pairs={{0,384},{128,0},{256,128},{384,256},{1,385},{129,1},{257,129},{385... | collective-permute-start | bytes 1474568 | tf_op jit(solution)/shard_map/ppermute | solution.py:155
  51.1 23.0 %all-to-all-start.1 = ((bf16[16,32,896]{2,1,0:T(8,128)(2,1)}), bf16[16,32,896]{2,1,0:T(8,128)(2,1)}, u32[]{:S(2)}, u32[]{:S(2)}) async-start(bf16[16,32,896]{2,1,0:T(8,128)(2,1)} %shard_map.103), calls=%async_computation.1 | async-start | bytes 1835008 | tf_op jit(solution)/shard_map/all_to_all | solution.py:162
  60.1 0.8 copy-start.4
  60.9 1.0 copy-start.5
  75.7 3.7 %collective-permute-start.3 = (bf16[256,896]{1,0:T(8,128)(2,1)S(1)}, bf16[256,896]{1,0:T(8,128)(2,1)S(1)}, u32[]{:S(2)}, u32[]{:S(2)}) collective-permute-start(bf16[256,896]{1,0:T(8,128)(2,1)S(1)} %fusion), channel_id=1, source_target_pairs={{0,64},{64,0},{1,65},{65,1},{2,66},{66,2},{3,67},{67,3},{4,68},{68... | collective-permute-start | bytes 1376264 | tf_op jit(solution)/shard_map/ppermute | solution.py:174
  81.1 22.7 %copy-start.1 = (f32[1,32,3584]{2,1,0:T(8,128)S(1)}, f32[1,32,3584]{2,1,0:T(8,128)}, u32[]{:S(2)}) copy-start(f32[1,32,3584]{2,1,0:T(8,128)} %weight_ref.1) | copy-start | bytes 1376260
  81.1 22.7 %copy-start.2 = (bf16[1,32,3584]{2,1,0:T(8,128)(2,1)S(1)}, bf16[1,32,3584]{2,1,0:T(8,128)(2,1)}, u32[]{:S(2)}) copy-start(bf16[1,32,3584]{2,1,0:T(8,128)(2,1)} %moment_ref.1) | copy-start | bytes 688132
  81.1 22.7 %copy-start.3 = (bf16[1,32,3584]{2,1,0:T(8,128)(2,1)S(1)}, bf16[1,32,3584]{2,1,0:T(8,128)(2,1)}, u32[]{:S(2)}) copy-start(bf16[1,32,3584]{2,1,0:T(8,128)(2,1)} %second_ref.1) | copy-start | bytes 688132
